TPU v7x, 32 devices: a whole 2x2x4 slice. The times are simulated.
32 devices in a mesh: seq: 8 (over z, y), head: 4 (over x, core).
Axes of the slice: x: 2, y: 2, z: 4, core: 2. Of those that a mesh axis runs over, the one named last changes fastest.
Arguments:
- tokens: bfloat16 [16, 196, 768], P('seq'), may hold values from -6 to 6
- cls_tokens: bfloat16 [4, 768], replicated, may hold values from -6 to 6
- clip_lengths: int32 [4], replicated, may hold values from 1 to 8, 16 in all
- time_gain: float32 [768], replicated, may hold values from 0.1 to 1.9
- time_beta: float32 [768], replicated, may hold values from -1.75 to 1.75
- time_proj_in: bfloat16 [768, 3, 768], P(None, None, 'head'), may hold values from -0.21875 to 0.21875
- time_qv_bias: float32 [2, 768], P(None, 'head'), may hold values from -1.75 to 1.75
- time_proj_out: bfloat16 [768, 768], P('head'), may hold values from -0.3125 to 0.3125
- time_out_bias: float32 [768], replicated, may hold values from -1.75 to 1.75
- time_linear: bfloat16 [768, 768], replicated, may hold values from -0.21875 to 0.21875
- time_linear_bias: float32 [768], replicated, may hold values from -1.75 to 1.75
- space_gain: float32 [768], replicated, may hold values from 0.1 to 1.9
- space_beta: float32 [768], replicated, may hold values from -1.75 to 1.75
- space_proj_in: bfloat16 [768, 3, 768], P(None, None, 'head'), may hold values from -0.21875 to 0.21875
- space_qv_bias: float32 [2, 768], P(None, 'head'), may hold values from -1.75 to 1.75
- space_proj_out: bfloat16 [768, 768], P('head'), may hold values from -0.625 to 0.625
- space_out_bias: float32 [768], replicated, may hold values from -1.75 to 1.75
- mlp_gain: float32 [768], replicated, may hold values from 0.1 to 1.9
- mlp_beta: float32 [768], replicated, may hold values from -1.75 to 1.75
- mlp_up: bfloat16 [768, 3072], P(None, 'head'), may hold values from -0.21875 to 0.21875
- mlp_up_bias: float32 [3072], P('head'), may hold values from -1.75 to 1.75
- mlp_down: bfloat16 [3072, 768], P('head'), may hold values from -0.109375 to 0.109375
- mlp_down_bias: float32 [768], replicated, may hold values from -1.75 to 1.75
- out_grad: bfloat16 [16, 196, 768], P('seq'), may hold values from -6 to 6
- cls_grad: bfloat16 [4, 768], replicated, may hold values from -6 to 6
Outputs:
- block_out: bfloat16 [16, 196, 768], P('seq')
- cls_out: bfloat16 [4, 768], replicated
- tokens_grad: bfloat16 [16, 196, 768], P('seq')
- cls_tokens_grad: float32 [4, 768], P(None, 'seq')
- time_gain_grad: float32 [768], P('seq')
- time_beta_grad: float32 [768], replicated
- time_proj_in_grad: float32 [768, 3, 768], P('seq', None, 'head')
- time_qv_bias_grad: float32 [2, 768], P(None, 'head')
- time_proj_out_grad: float32 [768, 768], P('head', 'seq')
- time_out_bias_grad: float32 [768], replicated
- time_linear_grad: float32 [768, 768], P('seq', 'head')
- time_linear_bias_grad: float32 [768], replicated
- space_gain_grad: float32 [768], P('seq')
- space_beta_grad: float32 [768], replicated
- space_proj_in_grad: float32 [768, 3, 768], P('seq', None, 'head')
- space_qv_bias_grad: float32 [2, 768], P(None, 'head')
- space_proj_out_grad: float32 [768, 768], P('head', 'seq')
- space_out_bias_grad: float32 [768], replicated
- mlp_gain_grad: float32 [768], P('seq')
- mlp_beta_grad: float32 [768], replicated
- mlp_up_grad: float32 [768, 3072], P('seq', 'head')
- mlp_up_bias_grad: float32 [3072], P('head')
- mlp_down_grad: float32 [3072, 768], P('head', 'seq')
- mlp_down_bias_grad: float32 [768], replicated
Inputs may be any that keep to these rules, and one draw needn't show every extreme that they name: clip_lengths sum to 16; some clip has exactly 8 frames.
All inputs are finite; a program needn't handle non-finite values.
Results may differ from a plain program's by a relative error of at most 0.035.
Values may be sent and summed in bfloat16 or wider, within the bound.
A program may use at most 128 MiB of HBM per device.

v0:
```python
import jax
import jax.numpy as jnp
from jax import lax
from jax.sharding import PartitionSpec as P

HEAD_DIM = 64
PATCH = 196
MAXLEN = 8


EPS = 1e-06
NEG = -1e30
FLOAT = jnp.float32
BHALF = jnp.bfloat16


def matmul_plain(left, right):
    return jnp.dot(left, right, preferred_element_type=FLOAT)


def matmul_tn(left, right):
    return lax.dot_general(left, right, (((0,), (0,)), ((), ())), preferred_element_type=FLOAT)


def matmul_nt(left, right):
    return lax.dot_general(left, right, (((1,), (1,)), ((), ())), preferred_element_type=FLOAT)


def exact_tn(left, right):
    return lax.dot_general(
        left,
        right,
        (((0,), (0,)), ((), ())),
        precision=lax.Precision.HIGHEST,
        preferred_element_type=FLOAT,
    )


def exact_nn(left, right):
    return jnp.dot(left, right, precision=lax.Precision.HIGHEST, preferred_element_type=FLOAT)


def layer_norm(rows, gain, shift):
    center = rows - jnp.mean(rows, axis=-1, keepdims=True)
    invstd = lax.rsqrt(jnp.mean(center * center, axis=-1, keepdims=True) + EPS)
    normed = center * invstd
    return (normed * gain + shift, normed, invstd)


def norm_back(grad_out, gain, normed, invstd, row_weight):
    feature_count = grad_out.shape[-1]
    grad_norm = grad_out * gain
    weighted = grad_out * row_weight
    gain_grad = jnp.sum((weighted * normed).reshape(-1, feature_count), axis=0)
    shift_grad = jnp.sum(weighted.reshape(-1, feature_count), axis=0)
    first_mean = jnp.mean(grad_norm, axis=-1, keepdims=True)
    second_mean = jnp.mean(grad_norm * normed, axis=-1, keepdims=True)
    return (invstd * (grad_norm - first_mean - normed * second_mean), gain_grad, shift_grad)


def qkv_shift(pair):
    return jnp.stack([pair[0], jnp.zeros_like(pair[0]), pair[1]], axis=0).reshape(-1)


def pair_sums(grad_qkv, local_width):
    sums = jnp.sum(grad_qkv.astype(FLOAT).reshape(-1, 3, local_width), axis=0)
    return jnp.stack([sums[0], sums[2]], axis=0)


def gelu_slope(pre):
    normal_cdf = 0.5 * (1.0 + jax.scipy.special.erf(pre * 0.7071067811865476))
    return normal_cdf + pre * jnp.exp(-0.5 * pre * pre) * 0.3989422804014327


def band_stack(values, band_reach):
    frames = values.shape[0]
    padded = jnp.pad(values, ((band_reach, band_reach),) + ((0, 0),) * (values.ndim - 1))
    return jnp.stack(
        [padded[offset : offset + frames] for offset in range(2 * band_reach + 1)], axis=2
    )


def band_return(contrib, band_reach):
    frames = contrib.shape[0]
    padded = jnp.pad(contrib, ((band_reach, band_reach),) + ((0, 0),) * (contrib.ndim - 1))
    total = jnp.zeros((frames,) + contrib.shape[1:2] + contrib.shape[3:], FLOAT)
    for offset in range(2 * band_reach + 1):
        start = 2 * band_reach - offset
        total = total + padded[start : start + frames, :, offset]
    return total


def to_positions(frame_major):
    frames_dev, patches, columns = frame_major.shape
    seq_count = lax.axis_size("seq")
    pos_dev = (patches + seq_count - 1) // seq_count
    padded = jnp.pad(frame_major, ((0, 0), (0, pos_dev * seq_count - patches), (0, 0)))
    moved = lax.all_to_all(
        padded.reshape(frames_dev, seq_count, pos_dev, columns),
        "seq",
        split_axis=1,
        concat_axis=0,
        tiled=True,
    )
    return moved.reshape(frames_dev * seq_count, pos_dev, columns)


def to_frames(pos_major):
    frames_all, pos_dev, columns = pos_major.shape
    seq_count = lax.axis_size("seq")
    moved = lax.all_to_all(
        pos_major.reshape(frames_all, 1, pos_dev, columns),
        "seq",
        split_axis=0,
        concat_axis=1,
        tiled=True,
    )
    return moved.reshape(frames_all // seq_count, seq_count * pos_dev, columns)[:, :PATCH]


def head_cols(pieces):
    return lax.all_gather(pieces, "head", axis=2, tiled=True)


def time_scores(queries, key_band, valid, score_scale):
    raw = (
        jnp.einsum("fphd,fpohd->fpho", queries, key_band, preferred_element_type=FLOAT)
        * score_scale
    )
    return jnp.where(valid[:, None, None, :], raw, NEG)


def time_forward(queries, key_band, value_band, valid, score_scale):
    scores = time_scores(queries, key_band, valid, score_scale)
    largest = jnp.max(scores, axis=-1, keepdims=True)
    exponent = jnp.exp(scores - largest)
    totals = jnp.sum(exponent, axis=-1, keepdims=True)
    attend = (exponent / totals).astype(BHALF)
    result = jnp.einsum("fpho,fpohd->fphd", attend, value_band, preferred_element_type=FLOAT)
    return (result, largest + jnp.log(totals))


def time_backward(
    queries, key_band, value_band, valid, log_total, grad_out, score_scale, band_reach
):
    scores = time_scores(queries, key_band, valid, score_scale)
    attend = jnp.exp(scores - log_total)
    grad_attend = jnp.einsum("fphd,fpohd->fpho", grad_out, value_band, preferred_element_type=FLOAT)
    row_dot = jnp.sum(attend * grad_attend, axis=-1, keepdims=True)
    grad_score = (attend * (grad_attend - row_dot)).astype(BHALF)
    grad_query = (
        jnp.einsum("fpho,fpohd->fphd", grad_score, key_band, preferred_element_type=FLOAT)
        * score_scale
    )
    key_part = (
        jnp.einsum("fpho,fphd->fpohd", grad_score, queries, preferred_element_type=FLOAT)
        * score_scale
    )
    value_part = jnp.einsum(
        "fpho,fphd->fpohd", attend.astype(BHALF), grad_out, preferred_element_type=FLOAT
    )
    return (grad_query, band_return(key_part, band_reach), band_return(value_part, band_reach))


def space_forward(queries, key_rows, value_rows, score_scale):
    scores = (
        jnp.einsum("fqhd,fkhd->fhqk", queries, key_rows, preferred_element_type=FLOAT) * score_scale
    )
    largest = jnp.max(scores, axis=-1, keepdims=True)
    exponent = jnp.exp(scores - largest)
    totals = jnp.sum(exponent, axis=-1, keepdims=True)
    attend = (exponent / totals).astype(BHALF)
    result = jnp.einsum("fhqk,fkhd->fqhd", attend, value_rows, preferred_element_type=FLOAT)
    return (result, largest + jnp.log(totals))


def space_backward(queries, key_rows, value_rows, log_total, grad_out, score_scale):
    scores = (
        jnp.einsum("fqhd,fkhd->fhqk", queries, key_rows, preferred_element_type=FLOAT) * score_scale
    )
    attend = jnp.exp(scores - log_total)
    grad_attend = jnp.einsum("fqhd,fkhd->fhqk", grad_out, value_rows, preferred_element_type=FLOAT)
    row_dot = jnp.sum(attend * grad_attend, axis=-1, keepdims=True)
    grad_score = (attend * (grad_attend - row_dot)).astype(BHALF)
    grad_query = (
        jnp.einsum("fhqk,fkhd->fqhd", grad_score, key_rows, preferred_element_type=FLOAT)
        * score_scale
    )
    grad_key = (
        jnp.einsum("fhqk,fqhd->fkhd", grad_score, queries, preferred_element_type=FLOAT)
        * score_scale
    )
    grad_value = jnp.einsum(
        "fhqk,fqhd->fkhd", attend.astype(BHALF), grad_out, preferred_element_type=FLOAT
    )
    return (grad_query, grad_key, grad_value)


def body(
    tokens,
    cls_tokens,
    clip_lengths,
    time_gain,
    time_beta,
    time_proj_in,
    time_qv_bias,
    time_proj_out,
    time_out_bias,
    time_linear,
    time_linear_bias,
    space_gain,
    space_beta,
    space_proj_in,
    space_qv_bias,
    space_proj_out,
    space_out_bias,
    mlp_gain,
    mlp_beta,
    mlp_up,
    mlp_up_bias,
    mlp_down,
    mlp_down_bias,
    out_grad,
    cls_grad,
):
    frames_dev, patches, model_width = tokens.shape
    seq_count = lax.axis_size("seq")
    frames_all = frames_dev * seq_count
    clip_count = clip_lengths.shape[0]
    local_width = time_proj_in.shape[2]
    local_heads = local_width // HEAD_DIM
    band_reach = MAXLEN - 1
    score_scale = HEAD_DIM ** (-0.5)
    seq_rank = lax.axis_index("seq")
    head_rank = lax.axis_index("head")
    clip_ends = jnp.cumsum(clip_lengths)
    frame_ids = jnp.arange(frames_all, dtype=jnp.int32)
    clip_of = jnp.sum((frame_ids[:, None] >= clip_ends[None, :]).astype(jnp.int32), axis=1)
    clip_pad = jnp.pad(clip_of, (band_reach, band_reach), constant_values=-1)
    valid = jnp.stack(
        [clip_pad[offset : offset + frames_all] == clip_of for offset in range(2 * band_reach + 1)],
        axis=1,
    )
    local_clip = lax.dynamic_slice_in_dim(clip_of, seq_rank * frames_dev, frames_dev)
    onehot = (local_clip[:, None] == jnp.arange(clip_count, dtype=jnp.int32)[None, :]).astype(FLOAT)
    lengths = clip_lengths.astype(FLOAT)
    time_in = to_positions(tokens)
    pos_dev = time_in.shape[1]
    time_rows = frames_all * pos_dev
    time_normed, time_stat, time_inv = layer_norm(time_in.astype(FLOAT), time_gain, time_beta)
    time_normed = time_normed.astype(BHALF).reshape(time_rows, model_width)
    time_in_mat = time_proj_in.reshape(model_width, 3 * local_width)
    time_qkv = (
        (matmul_plain(time_normed, time_in_mat) + qkv_shift(time_qv_bias))
        .astype(BHALF)
        .reshape(frames_all, pos_dev, 3, local_heads, HEAD_DIM)
    )
    time_query = time_qkv[:, :, 0]
    time_keys = band_stack(time_qkv[:, :, 1], band_reach)
    time_values = band_stack(time_qkv[:, :, 2], band_reach)
    time_att, time_log = time_forward(time_query, time_keys, time_values, valid, score_scale)
    time_att = time_att.astype(BHALF).reshape(time_rows, local_width)
    time_mid = (
        lax.psum(matmul_plain(time_att, time_proj_out).astype(jnp.bfloat16), "head").astype(
            jnp.float32
        )
        + time_out_bias
    ).astype(BHALF)
    col_start = head_rank * local_width
    linear_cols = lax.dynamic_slice_in_dim(time_linear, col_start, local_width, 1)
    linear_shift = lax.dynamic_slice_in_dim(time_linear_bias, col_start, local_width)
    time_part = (
        (matmul_plain(time_mid, linear_cols) + linear_shift)
        .astype(BHALF)
        .reshape(frames_all, pos_dev, local_width)
    )
    time_res = to_frames(head_cols(time_part))
    mid = tokens.astype(FLOAT) + time_res.astype(FLOAT)
    span_rows = patches + 1
    space_rows = frames_dev * span_rows
    cls_rows = matmul_plain(onehot.astype(BHALF), cls_tokens)
    space_in = jnp.concatenate([cls_rows[:, None, :], mid], axis=1)
    space_normed, space_stat, space_inv = layer_norm(space_in, space_gain, space_beta)
    space_normed = space_normed.astype(BHALF).reshape(space_rows, model_width)
    space_in_mat = space_proj_in.reshape(model_width, 3 * local_width)
    space_qkv = (
        (matmul_plain(space_normed, space_in_mat) + qkv_shift(space_qv_bias))
        .astype(BHALF)
        .reshape(frames_dev, span_rows, 3, local_heads, HEAD_DIM)
    )
    space_query = space_qkv[:, :, 0]
    space_keys = space_qkv[:, :, 1]
    space_values = space_qkv[:, :, 2]
    space_att, space_log = space_forward(space_query, space_keys, space_values, score_scale)
    space_att = space_att.astype(BHALF).reshape(space_rows, local_width)
    space_sum = (
        lax.psum(matmul_plain(space_att, space_proj_out).astype(jnp.bfloat16), "head").astype(
            jnp.float32
        )
        + space_out_bias
    ).reshape(frames_dev, span_rows, model_width)
    after = mid + space_sum[:, 1:]
    cls_part = exact_tn(onehot, space_sum[:, 0])
    cls_mid = cls_tokens.astype(FLOAT) + lax.psum(cls_part, "seq") / lengths[:, None]
    tok_rows = frames_dev * patches
    rows = jnp.concatenate([after.reshape(tok_rows, model_width), cls_mid], axis=0)
    mlp_normed, mlp_stat, mlp_inv = layer_norm(rows, mlp_gain, mlp_beta)
    mlp_normed = mlp_normed.astype(BHALF)
    pre = matmul_plain(mlp_normed, mlp_up) + mlp_up_bias
    act = jax.nn.gelu(pre, approximate=False).astype(BHALF)
    result = (
        rows
        + lax.psum(matmul_plain(act, mlp_down).astype(jnp.bfloat16), "head").astype(jnp.float32)
        + mlp_down_bias
    )
    block_out = result[:tok_rows].reshape(frames_dev, patches, model_width).astype(BHALF)
    cls_out = result[tok_rows:].astype(BHALF)
    first_seq = (seq_rank == 0).astype(FLOAT)
    keep_rows = jnp.concatenate(
        [jnp.ones((tok_rows, 1), FLOAT), jnp.ones((clip_count, 1), FLOAT) * first_seq], axis=0
    )
    keep_half = keep_rows.astype(BHALF)
    grad_rows = jnp.concatenate([out_grad.reshape(tok_rows, model_width), cls_grad], axis=0)
    down_grad = matmul_tn(act * keep_half, grad_rows)
    down_shift_grad = jnp.sum(grad_rows.astype(FLOAT) * keep_rows, axis=0)
    grad_pre = (matmul_nt(grad_rows, mlp_down) * gelu_slope(pre)).astype(BHALF)
    up_grad = matmul_tn(mlp_normed * keep_half, grad_pre)
    up_shift_grad = jnp.sum(grad_pre.astype(FLOAT) * keep_rows, axis=0)
    grad_mlp_norm = lax.psum(matmul_nt(grad_pre, mlp_up).astype(jnp.bfloat16), "head").astype(
        jnp.float32
    )
    grad_mlp_in, mlp_gain_grad, mlp_beta_grad = norm_back(
        grad_mlp_norm, mlp_gain, mlp_stat, mlp_inv, keep_rows
    )
    grad_total = grad_rows.astype(FLOAT) + grad_mlp_in
    grad_after = grad_total[:tok_rows].reshape(frames_dev, patches, model_width)
    grad_cls_mid = grad_total[tok_rows:]
    cls_share = exact_nn(onehot, grad_cls_mid / lengths[:, None])
    grad_space_sum = (
        jnp.concatenate([cls_share[:, None, :], grad_after], axis=1)
        .astype(BHALF)
        .reshape(space_rows, model_width)
    )
    space_out_grad = matmul_tn(space_att, grad_space_sum)
    space_shift_grad = jnp.sum(grad_space_sum.astype(FLOAT), axis=0)
    grad_space_att = (
        matmul_nt(grad_space_sum, space_proj_out)
        .astype(BHALF)
        .reshape(frames_dev, span_rows, local_heads, HEAD_DIM)
    )
    space_grad_query, space_grad_key, space_grad_value = space_backward(
        space_query, space_keys, space_values, space_log, grad_space_att, score_scale
    )
    grad_space_qkv = (
        jnp.stack([space_grad_query, space_grad_key, space_grad_value], axis=2)
        .astype(BHALF)
        .reshape(space_rows, 3 * local_width)
    )
    space_in_grad = matmul_tn(space_normed, grad_space_qkv).reshape(model_width, 3, local_width)
    space_pair_grad = pair_sums(grad_space_qkv, local_width)
    grad_space_norm = (
        lax.psum(matmul_nt(grad_space_qkv, space_in_mat).astype(jnp.bfloat16), "head")
        .astype(jnp.float32)
        .reshape(frames_dev, span_rows, model_width)
    )
    grad_space_in, space_gain_grad, space_beta_grad = norm_back(
        grad_space_norm, space_gain, space_stat, space_inv, 1.0
    )
    grad_mid = grad_after + grad_space_in[:, 1:]
    cls_in_part = exact_tn(onehot, grad_space_in[:, 0])
    grad_time_res = to_positions(grad_mid.astype(BHALF)).reshape(time_rows, model_width)
    linear_grad = matmul_tn(
        time_mid, lax.dynamic_slice_in_dim(grad_time_res, col_start, local_width, 1)
    )
    linear_shift_grad = jnp.sum(grad_time_res.astype(FLOAT), axis=0)
    grad_time_mid = matmul_nt(grad_time_res, time_linear).astype(BHALF)
    time_out_grad = matmul_tn(time_att, grad_time_mid)
    time_shift_grad = jnp.sum(grad_time_mid.astype(FLOAT), axis=0)
    grad_time_att = (
        matmul_nt(grad_time_mid, time_proj_out)
        .astype(BHALF)
        .reshape(frames_all, pos_dev, local_heads, HEAD_DIM)
    )
    time_grad_query, time_grad_key, time_grad_value = time_backward(
        time_query, time_keys, time_values, valid, time_log, grad_time_att, score_scale, band_reach
    )
    grad_time_qkv = (
        jnp.stack([time_grad_query, time_grad_key, time_grad_value], axis=2)
        .astype(BHALF)
        .reshape(time_rows, 3 * local_width)
    )
    time_in_grad = matmul_tn(time_normed, grad_time_qkv).reshape(model_width, 3, local_width)
    time_pair_grad = pair_sums(grad_time_qkv, local_width)
    grad_time_norm = (
        lax.psum(matmul_nt(grad_time_qkv, time_in_mat).astype(jnp.bfloat16), "head")
        .astype(jnp.float32)
        .reshape(frames_all, pos_dev, model_width)
    )
    grad_time_in, time_gain_grad, time_beta_grad = norm_back(
        grad_time_norm, time_gain, time_stat, time_inv, 1.0
    )
    grad_tokens_time = to_frames(grad_time_in.astype(BHALF))
    tokens_grad = (grad_mid + grad_tokens_time.astype(FLOAT)).astype(BHALF)
    summed = (
        lax.psum_scatter(time_gain_grad, "seq", scatter_dimension=0, tiled=True),
        lax.psum_scatter(time_in_grad, "seq", scatter_dimension=0, tiled=True),
        lax.psum_scatter(time_out_grad, "seq", scatter_dimension=1, tiled=True),
        lax.psum_scatter(linear_grad, "seq", scatter_dimension=0, tiled=True),
        lax.psum_scatter(space_gain_grad, "seq", scatter_dimension=0, tiled=True),
        lax.psum_scatter(space_in_grad, "seq", scatter_dimension=0, tiled=True),
        lax.psum_scatter(space_out_grad, "seq", scatter_dimension=1, tiled=True),
        lax.psum_scatter(mlp_gain_grad, "seq", scatter_dimension=0, tiled=True),
        lax.psum_scatter(up_grad, "seq", scatter_dimension=0, tiled=True),
        lax.psum_scatter(down_grad, "seq", scatter_dimension=1, tiled=True),
        lax.psum_scatter(cls_in_part, "seq", scatter_dimension=1, tiled=True),
    )
    shifts = lax.psum(
        (
            time_beta_grad,
            time_pair_grad,
            time_shift_grad,
            linear_shift_grad,
            space_beta_grad,
            space_pair_grad,
            space_shift_grad,
            mlp_beta_grad,
            up_shift_grad,
            down_shift_grad,
        ),
        "seq",
    )
    col_width = model_width // seq_count
    cls_direct = lax.dynamic_slice_in_dim(grad_cls_mid, seq_rank * col_width, col_width, 1)
    cls_tokens_grad = summed[10] + cls_direct
    return (
        block_out,
        cls_out,
        tokens_grad,
        cls_tokens_grad,
        summed[0],
        shifts[0],
        summed[1],
        shifts[1],
        summed[2],
        shifts[2],
        summed[3],
        shifts[3],
        summed[4],
        shifts[4],
        summed[5],
        shifts[5],
        summed[6],
        shifts[6],
        summed[7],
        shifts[7],
        summed[8],
        shifts[8],
        summed[9],
        shifts[9],
    )


def solution(mesh):
    placed = (
        P("seq", None, None),
        P(),
        P(),
        P(),
        P(),
        P(None, None, "head"),
        P(None, "head"),
        P("head", None),
        P(),
        P(),
        P(),
        P(),
        P(),
        P(None, None, "head"),
        P(None, "head"),
        P("head", None),
        P(),
        P(),
        P(),
        P(None, "head"),
        P("head"),
        P("head", None),
        P(),
        P("seq", None, None),
        P(),
    )
    return jax.shard_map(
        body,
        mesh=mesh,
        in_specs=placed,
        out_specs=(
            P("seq", None, None),
            P(),
            P("seq", None, None),
            P(None, "seq"),
            P("seq"),
            P(),
            P("seq", None, "head"),
            P(None, "head"),
            P("head", "seq"),
            P(),
            P("seq", "head"),
            P(),
            P("seq"),
            P(),
            P("seq", None, "head"),
            P(None, "head"),
            P("head", "seq"),
            P(),
            P("seq"),
            P(),
            P("seq", "head"),
            P("head"),
            P("head", "seq"),
            P(),
        ),
        check_vma=False,
    )
```

profile of v0, /device:TPU:0, one launch (start us, length us, event | category | flops | bytes accessed | tf_op | source)
XLA Modules:
  0.0 1067.6 jit_solution(7240975503798920468)
XLA Ops:
  7.2 2.5 pad.27
  9.7 7.4 all-to-all-start
  18.0 15.5 %all-to-all-done = bf16[2,8,25,768]{3,0,2,1:T(2,128)(2,1)S(1)} async-done(((bf16[2,8,25,768]{3,0,2,1:T(2,128)(2,1)}), bf16[2,8,25,768]{3,0,2,1:T(2,128)(2,1)S(1)}, u32[]{:S(2)}, u32[]{:S(2)}) %all-to-all-start) | async-done | bytes 614432 | tf_op jit(solution)/shard_map/all_to_all | solution.py:98
  52.4 2.6 copy-done.51
  55.0 3.3 fusion.7
  58.3 4.1 copy.697
  62.4 3.2 fusion.29
  67.1 3.0 fusion.16
  70.2 6.6 copy.698
  76.8 4.2 fusion.3
  83.9 32.0 %all-reduce.19.cloned.1.call-done = bf16[400,768]{1,0:T(8,128)(2,1)} async-done(((bf16[400,768]{1,0:T(8,128)(2,1)}), bf16[400,768]{1,0:T(8,128)(2,1)}) %all-reduce.19.cloned.1.call-update) | async-done | bytes 614416 | tf_op jit(solution)/shard_map/psum | solution.py:264
  118.8 20.7 %all_gather.3 = bf16[16,25,768]{1,0,2:T(8,128)(2,1)} all-gather(bf16[16,25,192]{1,0,2:T(8,128)(2,1)S(1)} %reshape.683), channel_id=1, replica_groups=mesh['seq'=8,'head'=4] {'head'}, dimensions={2}, use_global_device_ids=true | all-gather | bytes 768000 | tf_op jit(solution)/shard_map/all_gather | solution.py:122
  139.4 5.3 copy.654
  144.8 6.0 all-to-all-start.1
  151.3 20.2 %all-to-all-done.1 = bf16[16,1,25,768]{3,2,1,0:T(8,128)(2,1)} async-done(((bf16[16,1,25,768]{3,2,1,0:T(8,128)(2,1)}), bf16[16,1,25,768]{3,2,1,0:T(8,128)(2,1)}, u32[]{:S(2)}, u32[]{:S(2)}) %all-to-all-start.1) | async-done | bytes 614432 | tf_op jit(solution)/shard_map/all_to_all | solution.py:111
  183.0 2.4 fusion.185
  194.0 28.9 %all-reduce.21.cloned.1.call-done = bf16[394,768]{1,0:T(8,128)(2,1)} async-done(((bf16[394,768]{1,0:T(8,128)(2,1)}), bf16[394,768]{1,0:T(8,128)(2,1)}) %all-reduce.21.cloned.1.call-update) | async-done | bytes 605200 | tf_op jit(solution)/shard_map/psum | solution.py:297
  225.1 2.4 reshape.658
  233.7 37.1 %psum.121 = f32[4,768]{1,0:T(4,128)S(1)} all-reduce(f32[4,768]{1,0:T(4,128)S(1)} %fusion.169), channel_id=1, replica_groups=mesh['seq'=8,'head'=4] {'seq'}, use_global_device_ids=true, to_apply=%region_12.13 | all-reduce | flops 3072 | bytes 24576 | tf_op jit(solution)/shard_map/psum | solution.py:304
  272.3 4.3 fusion.39
  280.3 29.6 %all-reduce.23.cloned.1.call-done = bf16[396,768]{1,0:T(8,128)(2,1)} async-done(((bf16[396,768]{1,0:T(8,128)(2,1)}), bf16[396,768]{1,0:T(8,128)(2,1)}) %all-reduce.23.cloned.1.call-update) | async-done | bytes 608272 | tf_op jit(solution)/shard_map/psum | solution.py:329
  310.0 2.5 fusion.33
  314.7 2.4 reshape.661
  317.1 2.4 convert_reduce_fusion.1
  329.5 2.8 convert_element_type.335
  332.3 2.9 convolution_convert_fusion.2
  335.2 2.5 copy.679
  337.9 2.5 concatenate.21
  340.5 28.5 %all-reduce.25.cloned.1.call-done = bf16[394,768]{1,0:T(8,128)(2,1)} async-done(((bf16[394,768]{1,0:T(8,128)(2,1)}), bf16[394,768]{1,0:T(8,128)(2,1)}) %all-reduce.25.cloned.1.call-update) | async-done | bytes 605200 | tf_op jit(solution)/shard_map/psum | solution.py:362
  373.8 4.5 fusion.53
  380.7 5.5 all-to-all-start.2
  386.2 2.9 convolution_convert_fusion.4
  389.2 12.8 %all-to-all-done.2 = bf16[2,8,25,768]{3,0,2,1:T(2,128)(2,1)} async-done(((bf16[2,8,25,768]{3,0,2,1:T(2,128)(2,1)}), bf16[2,8,25,768]{3,0,2,1:T(2,128)(2,1)}, u32[]{:S(2)}, u32[]{:S(2)}) %all-to-all-start.2) | async-done | bytes 614432 | tf_op jit(solution)/shard_map/all_to_all | solution.py:98
  411.3 6.5 fusion.1
  417.7 5.0 copy.706
  422.7 9.2 fusion.191
  431.9 7.2 copy.707
  439.1 4.5 fusion.5
  444.7 7.6 multiply_bitcast_fusion.1
  454.2 7.5 multiply_bitcast_fusion
  463.3 2.5 convert_reduce_fusion
  465.8 2.7 convert_element_type.344
  468.6 2.6 convolution_convert_fusion
  473.4 2.4 convolution_bitcast_fusion
  476.0 2.4 convolution_bitcast_fusion.1
  478.4 2.5 fusion.98
  483.1 3.6 fusion.193
  487.4 3.5 fusion.95
  491.0 3.4 fusion.93
  497.7 3.4 fusion.192
  507.1 2.7 reshape.669
  510.0 2.5 reshape.666
  514.6 3.2 fusion.90
  517.8 3.7 all-to-all-start.3
  521.5 55.4 %reduce-scatter.25.cloned.1.call-done = f32[96,4]{1,0:T(8,128)} async-done(((f32[768,4]{1,0:T(8,128)}), f32[96,4]{1,0:T(8,128)}) %reduce-scatter.25.cloned.1.call-update) | async-done | bytes 1552
  578.5 63.7 %reduce-scatter.29.cloned.1.call-done = f32[96,192]{1,0:T(8,128)} async-done(((f32[768,192]{1,0:T(8,128)}), f32[96,192]{1,0:T(8,128)}) %reduce-scatter.29.cloned.1.call-update) | async-done | bytes 73744
  646.5 36.8 %all-reduce.11 = (f32[768]{0:T(1024)S(1)}, f32[768]{0:T(1024)}, f32[2,192]{1,0:T(2,128)}, f32[768]{0:T(1024)}, f32[768]{0:T(1024)}, /*index=5*/f32[768]{0:T(1024...) all-reduce(f32[768]{0:T(1024)S(1)} %get-tuple-element.266, ...), channel_id=3, replica_groups=mesh['seq'=8,'head'=4] {'seq'}, use_global_device_ids=true, to_apply=%region_29.30.clone | all-reduce | flops 9216 | bytes 73728
  686.4 20.5 %reduce-scatter.27.cloned.1.call-done = f32[96,192]{1,0:T(8,128)} async-done(((f32[768,192]{1,0:T(8,128)}), f32[96,192]{1,0:T(8,128)}) %reduce-scatter.27.cloned.1.call-update) | async-done | bytes 73744
  709.3 3.6 add_convert_fusion.5
  712.9 59.8 %reduce-scatter.17.cloned.1.call-done = f32[96,192]{1,0:T(8,128)} async-done(((f32[768,192]{1,0:T(8,128)}), f32[96,192]{1,0:T(8,128)}) %reduce-scatter.17.cloned.1.call-update) | async-done | bytes 73744 | tf_op jit(solution)/shard_map/reduce_scatter | solution.py:408
  772.7 71.8 %reduce-scatter.19.cloned.1.call-done = f32[96,3,192]{2,0,1:T(8,128)} async-done(((f32[768,3,192]{2,0,1:T(8,128)}), f32[96,3,192]{2,0,1:T(8,128)}) %reduce-scatter.19.cloned.1.call-update) | async-done | bytes 221200 | tf_op jit(solution)/shard_map/reduce_scatter | solution.py:410
  844.5 72.2 %reduce-scatter.21.cloned.1.call-done = f32[96,768]{1,0:T(8,128)} async-done(((f32[768,768]{1,0:T(8,128)}), f32[96,768]{1,0:T(8,128)}) %reduce-scatter.21.cloned.1.call-update) | async-done | bytes 294928 | tf_op jit(solution)/shard_map/reduce_scatter | solution.py:413
  916.7 72.1 %reduce-scatter.23.cloned.1.call-done = f32[768,96]{0,1:T(8,128)} async-done(((f32[768,768]{0,1:T(8,128)}), f32[768,96]{0,1:T(8,128)}) %reduce-scatter.23.cloned.1.call-update) | async-done | bytes 294928 | tf_op jit(solution)/shard_map/reduce_scatter | solution.py:414
  988.8 72.0 %reduce-scatter.15.cloned.1.call-done = f32[96,3,192]{2,0,1:T(8,128)} async-done(((f32[768,3,192]{2,0,1:T(8,128)}), f32[96,3,192]{2,0,1:T(8,128)}) %reduce-scatter.15.cloned.1.call-update) | async-done | bytes 221200 | tf_op jit(solution)/shard_map/reduce_scatter | solution.py:406
  (367 shorter events, 121.2 us)
Async XLA Ops:
  7.2 264.8 %copy-start = (bf16[768,768]{1,0:T(8,128)(2,1)S(1)}, bf16[768,768]{1,0:T(8,128)(2,1)}, u32[]{:S(2)}) copy-start(bf16[768,768]{1,0:T(8,128)(2,1)} %param.44) | copy-start | bytes 3538948
  7.2 10.0 copy-start.63
  7.2 10.0 copy-start.62
  7.2 10.2 copy-start.73
  9.7 24.7 %copy-start.44 = (f32[768]{0:T(1024)S(1)}, f32[768]{0:T(1024)}, u32[]{:S(2)}) copy-start(f32[768]{0:T(1024)} %param.28) | copy-start | bytes 9220
  9.7 24.7 %copy-start.58 = (f32[768]{0:T(1024)S(1)}, f32[768]{0:T(1024)}, u32[]{:S(2)}) copy-start(f32[768]{0:T(1024)} %param.29) | copy-start | bytes 9220
  9.7 23.8 %all-to-all-start = ((bf16[2,8,25,768]{3,0,2,1:T(2,128)(2,1)}), bf16[2,8,25,768]{3,0,2,1:T(2,128)(2,1)S(1)}, u32[]{:S(2)}, u32[]{:S(2)}) async-start(bf16[2,8,25,768]{3,0,2,1:T(2,128)(2,1)} %bitcast.16), calls=%async_computation | async-start | bytes 1228800 | tf_op jit(solution)/shard_map/all_to_all | solution.py:98
  17.1 98.7 %all-reduce.19.cloned.1.call-start = ((), (), s32[]{:S(2)}) async-start(), calls=%async_computation.12 | async-start | bytes 1228800 | tf_op jit(solution)/shard_map/psum | solution.py:264
  18.0 49.1 %copy-start.46 = (pred[16,15]{1,0:T(8,128)(4,1)}, pred[16,15]{1,0:T(8,128)(4,1)S(1)}, u32[]{:S(2)}) copy-start(pred[16,15]{1,0:T(8,128)(4,1)S(1)} %copy.617) | copy-start | bytes 724
  34.8 3.2 copy-start.13
  49.7 2.6 copy-start.50
  52.4 2.6 copy-start.51
  62.3 3.2 copy-start.2
  67.1 3.0 copy-start.37
  81.1 34.7 %copy-start.69 = (f32[768]{0:T(1024)S(1)}, f32[768]{0:T(1024)}, u32[]{:S(2)}) copy-start(f32[768]{0:T(1024)} %param.33) | copy-start | bytes 9220
  81.9 33.9 %copy-start.27 = (bf16[400,192]{1,0:T(8,128)(2,1)}, bf16[400,192]{1,0:T(8,128)(2,1)S(1)}, u32[]{:S(2)}) copy-start(bf16[400,192]{1,0:T(8,128)(2,1)S(1)} %reshape.651) | copy-start | bytes 460804
  144.8 6.4 copy-start.57
  144.8 29.4 %copy-start.16 = (bf16[2,196,768]{2,0,1:T(2,128)(2,1)S(1)}, bf16[2,196,768]{2,0,1:T(2,128)(2,1)}, u32[]{:S(2)}) copy-start(bf16[2,196,768]{2,0,1:T(2,128)(2,1)} %param.25) | copy-start | bytes 1806340
  144.8 26.8 %all-to-all-start.1 = ((bf16[16,1,25,768]{3,2,1,0:T(8,128)(2,1)}), bf16[16,1,25,768]{3,2,1,0:T(8,128)(2,1)}, u32[]{:S(2)}, u32[]{:S(2)}) async-start(bf16[16,1,25,768]{3,2,1,0:T(8,128)(2,1)} %copy.654), calls=%async_computation.1 | async-start | bytes 1572864 | tf_op jit(solution)/shard_map/all_to_all | solution.py:111
  150.8 72.2 %all-reduce.21.cloned.1.call-start = ((), (), s32[]{:S(2)}) async-start(), calls=%async_computation.13 | async-start | bytes 1228800 | tf_op jit(solution)/shard_map/psum | solution.py:297
  151.1 82.4 %copy-start.64 = (s32[2]{0:T(128)}, s32[2]{0:T(128)S(1)}, u32[]{:S(2)}) copy-start(s32[2]{0:T(128)S(1)} %dynamic_slice.17) | copy-start | bytes 28
  175.5 2.6 copy-start.5
  178.3 3.1 copy-start.15
  190.2 119.8 %all-reduce.23.cloned.1.call-start = ((), (), s32[]{:S(2)}) async-start(), calls=%async_computation.14 | async-start | bytes 1228800 | tf_op jit(solution)/shard_map/psum | solution.py:329
  191.9 31.0 %copy-start.60 = (f32[768]{0:T(1024)S(1)}, f32[768]{0:T(1024)}, u32[]{:S(2)}) copy-start(f32[768]{0:T(1024)} %param.41) | copy-start | bytes 9220
  194.0 33.6 %copy-start.9 = (bf16[396,768]{1,0:T(8,128)(2,1)}, bf16[396,768]{1,0:T(8,128)(2,1)S(1)}, u32[]{:S(2)}) copy-start(bf16[396,768]{1,0:T(8,128)(2,1)S(1)} %constant_dynamic-update-slice_fusion) | copy-start | bytes 1824772
  227.6 2.3 copy-start.17
  227.6 2.3 copy-start.19
  272.3 4.3 copy-start.52
  272.3 4.3 copy-start.10
  272.3 4.3 copy-start.67
  279.8 89.2 %all-reduce.25.cloned.1.call-start = ((), (), s32[]{:S(2)}) async-start(), calls=%async_computation.15 | async-start | bytes 1228800 | tf_op jit(solution)/shard_map/psum | solution.py:362
  280.3 32.2 %copy-start.11 = (bf16[396,768]{1,0:T(8,128)(2,1)S(1)}, bf16[396,768]{1,0:T(8,128)(2,1)}, u32[]{:S(2)}) copy-start(bf16[396,768]{1,0:T(8,128)(2,1)} %copy-done.9) | copy-start | bytes 1824772
  280.3 32.2 %copy-start.53 = (f32[396]{0:T(512)S(1)}, f32[396]{0:T(512)}, u32[]{:S(2)}) copy-start(f32[396]{0:T(512)} %copy-done.52) | copy-start | bytes 4756
  280.3 32.2 %copy-start.55 = (f32[768]{0:T(1024)S(1)}, f32[768]{0:T(1024)}, u32[]{:S(2)}) copy-start(f32[768]{0:T(1024)} %param.42) | copy-start | bytes 9220
  310.0 2.6 copy-start.23
  317.1 4.4 copy-start.34
  319.5 5.3 copy-start.40
  335.2 2.5 copy-start.32
  373.8 4.5 copy-start.6
  380.7 21.3 %all-to-all-start.2 = ((bf16[2,8,25,768]{3,0,2,1:T(2,128)(2,1)}), bf16[2,8,25,768]{3,0,2,1:T(2,128)(2,1)}, u32[]{:S(2)}, u32[]{:S(2)}) async-start(bf16[2,8,25,768]{3,0,2,1:T(2,128)(2,1)} %bitcast.411), calls=%async_computation.2 | async-start | bytes 1228800 | tf_op jit(solution)/shard_map/all_to_all | solution.py:98
  386.2 123.8 %all-reduce.27.cloned.1.call-start = ((), (), s32[]{:S(2)}) async-start(), calls=%async_computation.24 | async-start | bytes 2457600 | tf_op jit(solution)/shard_map/psum | solution.py:395
  406.3 3.1 copy-start.36
  417.7 5.0 copy-start.38
  417.7 5.0 copy-start.47
  439.1 4.7 copy-start.21
  471.2 2.2 copy-start.30
  471.2 105.7 %reduce-scatter.25.cloned.1.call-start = ((), (), s32[]{:S(2)}) async-start(), calls=%async_computation.21 | async-start | bytes 442368
  473.3 2.6 copy-start.28
  473.3 168.8 %reduce-scatter.29.cloned.1.call-start = ((), (), s32[]{:S(2)}) async-start(), calls=%async_computation.23 | async-start | bytes 884736
  475.9 2.5 copy-start.70
  475.9 231.1 %reduce-scatter.27.cloned.1.call-start = ((), (), s32[]{:S(2)}) async-start(), calls=%async_computation.22 | async-start | bytes 884736
  478.4 294.3 %reduce-scatter.17.cloned.1.call-start = ((), (), s32[]{:S(2)}) async-start(), calls=%async_computation.17 | async-start | bytes 884736 | tf_op jit(solution)/shard_map/reduce_scatter | solution.py:408
  481.0 363.5 %reduce-scatter.19.cloned.1.call-start = ((), (), s32[]{:S(2)}) async-start(), calls=%async_computation.18 | async-start | bytes 2654208 | tf_op jit(solution)/shard_map/reduce_scatter | solution.py:410
  486.7 430.0 %reduce-scatter.21.cloned.1.call-start = ((), (), s32[]{:S(2)}) async-start(), calls=%async_computation.19 | async-start | bytes 2654208 | tf_op jit(solution)/shard_map/reduce_scatter | solution.py:413
  490.9 497.8 %reduce-scatter.23.cloned.1.call-start = ((), (), s32[]{:S(2)}) async-start(), calls=%async_computation.20 | async-start | bytes 2654208 | tf_op jit(solution)/shard_map/reduce_scatter | solution.py:414
  494.4 566.4 %reduce-scatter.15.cloned.1.call-start = ((), (), s32[]{:S(2)}) async-start(), calls=%async_computation.16 | async-start | bytes 2654208 | tf_op jit(solution)/shard_map/reduce_scatter | solution.py:406
  509.8 2.6 copy-start.45
  510.0 2.5 copy-start.25
  517.8 60.1 %slice-start = ((f32[396,768]{1,0:T(8,128)}), f32[4,768]{1,0:T(4,128)S(1)}, s32[]{:S(2)}) async-start(f32[396,768]{1,0:T(8,128)} %copy-done.20), calls=%async_computation.25 | async-start | bytes 24576 | tf_op jit(solution)/shard_map/slice | solution.py:337
  517.8 127.9 %copy-start.42 = (bf16[396,768]{1,0:T(8,128)(2,1)S(1)}, bf16[396,768]{1,0:T(8,128)(2,1)}, u32[]{:S(2)}) copy-start(bf16[396,768]{1,0:T(8,128)(2,1)} %get-tuple-element.296) | copy-start | bytes 1824772
  517.8 127.9 %copy-start.61 = (f32[768]{0:T(1024)S(1)}, f32[768]{0:T(1024)}, u32[]{:S(2)}) copy-start(f32[768]{0:T(1024)} %param.47) | copy-start | bytes 9220
  517.8 190.8 %all-to-all-start.3 = ((bf16[16,1,25,768]{3,2,1,0:T(8,128)(2,1)}), bf16[16,1,25,768]{3,2,1,0:T(8,128)(2,1)S(1)}, u32[]{:S(2)}, u32[]{:S(2)}) async-start(bf16[16,1,25,768]{3,2,1,0:T(8,128)(2,1)} %fusion.90), calls=%async_computation.3 | async-start | bytes 1572864 | tf_op jit(solution)/shard_map/all_to_all | solution.py:111
  709.2 351.6 %copy-start.1 = (bf16[768,768]{1,0:T(8,128)(2,1)S(1)}, bf16[768,768]{1,0:T(8,128)(2,1)}, u32[]{:S(2)}) copy-start(bf16[768,768]{1,0:T(8,128)(2,1)} %param.44) | copy-start | bytes 3538948
  (29 other events, 33.5 us)
Sparse Core Ops, SparseCore 0:
  83.3 32.5 all-reduce.18
  190.3 32.5 all-reduce.20
  279.9 30.0 all-reduce.22
  335.3 33.6 all-reduce.24
  471.4 36.6 all-reduce.26
  511.6 65.3 reduce-scatter.24
  580.6 61.5 reduce-scatter.28
  645.5 61.4 reduce-scatter.26
  711.2 61.4 reduce-scatter.16
  776.6 67.8 reduce-scatter.18
  848.6 68.0 reduce-scatter.20
  920.6 68.0 reduce-scatter.22
  992.8 67.9 reduce-scatter.14
where the time goes:
time: 1070 us
  waiting for transfers between devices  655 us (61%)
  local copies, waits for them, and re-layouts  130 us (12%)
  blocking collectives  94.5 us (9%)
  matrix products  73.9 us (7%)
  other arithmetic  73.8 us (7%)
  starting transfers between devices  23.8 us (2%)
  between operations  16.2 us (2%)
    unnamed x16, waiting for transfers between devices  140 us
    reduce_scatter x1, waiting for transfers between devices, body(): lax.psum_scatter(up_grad, 'seq', scatter_dimension=0, tiled=True)  72.2 us
    reduce_scatter x1, waiting for transfers between devices, body(): lax.psum_scatter(down_grad, 'seq', scatter_dimension=1, tiled=True)  72.1 us
    reduce_scatter x1, waiting for transfers between devices, body(): lax.psum_scatter(time_in_grad, 'seq', scatter_dimension=0, tiled=True)  72 us
    reduce_scatter x1, waiting for transfers between devices, body(): lax.psum_scatter(space_in_grad, 'seq', scatter_dimension=0, tiled=True)  71.8 us
    reduce_scatter x1, waiting for transfers between devices, body(): lax.psum_scatter(linear_grad, 'seq', scatter_dimension=0, tiled=True)  59.8 us
    psum x1, blocking collectives, body(): lax.psum(cls_part, 'seq') / lengths[:, None]  37.1 us
    unnamed x1, blocking collectives  36.8 us
  transfers between devices with their start and end apart: 17, of which 15 were waited for; matrix products, arithmetic and copies ran while one was open for 7% of the time, Pallas kernels for 0%

commit v1 on v0

--- a/solution.py
+++ b/solution.py
@@ -1,6 +1,10 @@
+import functools
+
 import jax
 import jax.numpy as jnp
 from jax import lax
+from jax.experimental import pallas as pl
+from jax.experimental.pallas import tpu as pltpu
 from jax.sharding import PartitionSpec as P
 
 HEAD_DIM = 64
@@ -233,7 +237,9 @@
     score_scale = HEAD_DIM ** (-0.5)
     seq_rank = lax.axis_index("seq")
     head_rank = lax.axis_index("head")
-    clip_ends = jnp.cumsum(clip_lengths)
+    clip_ends = jnp.sum(
+        jnp.where(jnp.tri(clip_lengths.shape[0], dtype=bool), clip_lengths[None, :], 0), axis=1
+    )
     frame_ids = jnp.arange(frames_all, dtype=jnp.int32)
     clip_of = jnp.sum((frame_ids[:, None] >= clip_ends[None, :]).astype(jnp.int32), axis=1)
     clip_pad = jnp.pad(clip_of, (band_reach, band_reach), constant_values=-1)
@@ -460,6 +466,799 @@
     )
 
 
+MESH = pl.DeviceIdType.MESH
+ROWS = 208
+HALF = 16
+SLOTS = 2 * HALF
+BLOCK = 32
+
+
+def dot_nn(left, right):
+    return jnp.dot(left, right, preferred_element_type=FLOAT)
+
+
+def dot_nt(left, right):
+    return lax.dot_general(left, right, (((1,), (1,)), ((), ())), preferred_element_type=FLOAT)
+
+
+def dot_tn(left, right):
+    return lax.dot_general(left, right, (((0,), (0,)), ((), ())), preferred_element_type=FLOAT)
+
+
+def iota(shape, axis):
+    return lax.broadcasted_iota(jnp.int32, shape, axis)
+
+
+def scratch_shapes(dims):
+    frames, seq, width, model, hidden = dims["frames"], dims["seq"], dims["width"], dims["model"], dims["hidden"]
+    rows, every, heads = frames * ROWS, frames * seq, width // HEAD_DIM
+    half, low = model // 2, BHALF
+    vm = pltpu.VMEM
+    shapes = dict(
+        tok=vm((frames, dims["patches"], model), low),
+        out_grad=vm((frames, dims["patches"], model), low),
+        w_ti=vm((model, 3 * width), low),
+        w_si=vm((model, 3 * width), low),
+        w_tl=vm((model, model), low),
+        w_up=vm((model, hidden), low),
+        w_dn=vm((hidden, model), low),
+        w_to=vm((2, 2, width, model), low),
+        w_so=vm((2, 2, width, model), low),
+        x32=vm((rows, model), FLOAT),
+        gr32=vm((rows, model), FLOAT),
+        t32=vm((rows, model), FLOAT),
+        u32=vm((rows, model), FLOAT),
+        dact=vm((rows, hidden), FLOAT),
+        xh_t=vm((rows, model), FLOAT),
+        xh_s=vm((rows, model), FLOAT),
+        xh_m=vm((rows, model), FLOAT),
+        inv=vm((3, rows, 128), FLOAT),
+        n_t=vm((rows, model), low),
+        n_s=vm((rows, model), low),
+        n_m=vm((rows, model), low),
+        gr16=vm((rows, model), low),
+        mid16=vm((rows, model), low),
+        act=vm((rows, hidden), low),
+        act_k=vm((rows, hidden), low),
+        gpre=vm((rows, hidden), low),
+        gpre_k=vm((rows, hidden), low),
+        gss=vm((rows, model), low),
+        gtr=vm((rows, model), low),
+        gtm=vm((rows, model), low),
+        sqkv=vm((rows, 3 * width), low),
+        dsq=vm((rows, 3 * width), low),
+        dtq=vm((rows, 3 * width), low),
+        gatt=vm((rows, width), low),
+        sel=vm((seq * SLOTS, ROWS), low),
+        les=vm((ROWS, seq * SLOTS), low),
+        tmask=vm((every * HALF, every * HALF), FLOAT),
+        p_t=vm((2 * heads, every * HALF, every * HALF), FLOAT),
+        p_s=vm((frames * heads, ROWS, ROWS), FLOAT),
+        q_send=vm((seq, 2, frames, HALF, 3 * width), low),
+        q_pos=vm((2, every, HALF, 3 * width), low),
+        a_pos=vm((2, every, HALF, width), low),
+        a_recv=vm((seq, 2, frames, HALF, width), low),
+        g_send=vm((seq, 2, frames, HALF, width), low),
+        g_pos=vm((2, every, HALF, width), low),
+        d_pos=vm((2, every, HALF, 3 * width), low),
+        d_recv=vm((seq, 2, frames, HALF, 3 * width), low),
+        att_t=vm((2, 2, rows, width), low),
+        att_s=vm((2, 2, rows, width), low),
+        part=vm((4, 2, rows, half), low),
+        pair=vm((4, rows, half), low),
+        other=vm((4, rows, half), low),
+        total=vm((4, 2, rows, half), low),
+        cls_send=vm((8, model), FLOAT),
+        cls_recv=vm((seq, 8, model), FLOAT),
+        gcm=vm((8, model), FLOAT),
+        v_send=vm((3, 8, model), FLOAT),
+        v_recv=vm((3, seq, 8, model), FLOAT),
+    )
+    for name, columns in grad_columns(dims):
+        shapes["g_" + name] = vm((seq // 2, 2, model // seq, columns), low)
+        shapes["y_" + name] = vm((seq // 2, model // seq, columns), low)
+        shapes["z_" + name] = vm((seq // 2, model // seq, columns), low)
+    shapes["load"] = pltpu.SemaphoreType.DMA((16,))
+    shapes["sent"] = pltpu.SemaphoreType.DMA((160,))
+    shapes["got"] = pltpu.SemaphoreType.DMA((160,))
+    return shapes
+
+
+def grad_columns(dims):
+    width, model, hidden = dims["width"], dims["model"], dims["hidden"]
+    return (
+        ("dn", hidden),
+        ("up", hidden),
+        ("si", 3 * width),
+        ("so", width),
+        ("tl", width),
+        ("to", width),
+        ("ti", 3 * width),
+    )
+
+
+INPUTS = ("lens", "cls", "cls_grad", "vec", "h_tok", "h_og", "h_ti", "h_to", "h_tl", "h_si", "h_so", "h_up", "h_dn")
+OUTPUTS = ("o_blk", "o_cls", "o_tok", "o_vec")
+
+
+class Refs:
+    pass
+
+
+def layer_kernel(dims, names, *refs):
+    k = Refs()
+    for name, ref in zip(names, refs):
+        setattr(k, name, ref)
+    frames, seq, width, model, hidden = dims["frames"], dims["seq"], dims["width"], dims["model"], dims["hidden"]
+    patches, clips, pos = dims["patches"], dims["clips"], dims["pos"]
+    rows, every, heads, half = frames * ROWS, frames * seq, width // HEAD_DIM, model // 2
+    zs = seq // 2
+    scale = HEAD_DIM ** (-0.5)
+    s, h = lax.axis_index("seq"), lax.axis_index("head")
+    z, y = s // 2, s % 2
+    x, c = h // 2, h % 2
+    other_c = 1 - c
+    sister, across = (s, x * 2 + other_c), (s, (1 - x) * 2 + c)
+    y_peer = (z * 2 + 1 - y, h)
+    z_peers = [((z + i) % zs) for i in range(1, zs)]
+    peers = [((z + i) % zs) * 2 + (y + j) % 2 for i in range(zs) for j in range(2) if i or j]
+    used = [0]
+
+    def send(src, dst, device):
+        index = used[0]
+        used[0] += 1
+        copy = pltpu.make_async_remote_copy(
+            src_ref=src,
+            dst_ref=dst,
+            send_sem=k.sent.at[index],
+            recv_sem=k.got.at[index],
+            device_id=device,
+            device_id_type=MESH,
+        )
+        copy.start()
+        unsent.append(copy)
+        return copy
+
+    unsent = []
+    loads = [0]
+
+    def load(src, dst):
+        copy = pltpu.make_async_copy(src, dst, k.load.at[loads[0]])
+        loads[0] += 1
+        copy.start()
+        return copy
+
+    def blocks(body, unroll=False):
+        if unroll:
+            for i in range(rows // BLOCK):
+                body(pl.ds(i * BLOCK, BLOCK))
+        else:
+
+            def step(i, carry):
+                body(pl.ds(pl.multiple_of(i * BLOCK, BLOCK), BLOCK))
+                return carry
+
+            lax.fori_loop(0, rows // BLOCK, step, 0)
+
+    l_tok = load(k.h_tok, k.tok)
+    l_ti = load(k.h_ti, k.w_ti)
+    l_to = load(k.h_to, k.w_to.at[0, c])
+    l_so = load(k.h_so, k.w_so.at[0, c])
+    l_og = load(k.h_og, k.out_grad)
+    l_dn = load(k.h_dn, k.w_dn)
+    l_tl = load(k.h_tl, k.w_tl)
+    l_si = load(k.h_si, k.w_si)
+    l_up = load(k.h_up, k.w_up)
+    barrier = pltpu.get_barrier_semaphore()
+    everyone = [(p, h) for p in peers] + [sister, across]
+    for device in everyone:
+        pl.semaphore_signal(barrier, inc=1, device_id=device, device_id_type=MESH)
+
+    def vec(i):
+        return k.vec[i : i + 1, :]
+
+    t_gain, t_beta, t_ob, t_lb, s_gain, s_beta, s_ob, m_gain, m_beta, m_db, m_ub = [vec(i) for i in range(11)]
+    t_qb, s_qb = vec(11)[:, : 3 * width], vec(12)[:, : 3 * width]
+
+    slot, row = iota((seq * SLOTS, ROWS), 0), iota((seq * SLOTS, ROWS), 1)
+    place = (slot // SLOTS) * pos + slot % SLOTS
+    k.sel[...] = jnp.where((place == row) & (slot % SLOTS < pos) & (row < patches), 1.0, 0.0).astype(BHALF)
+    row, slot = iota((ROWS, seq * SLOTS), 0), iota((ROWS, seq * SLOTS), 1)
+    place = (slot // SLOTS) * pos + slot % SLOTS
+    k.les[...] = jnp.where((place == row) & (slot % SLOTS < pos) & (row < patches), 1.0, 0.0).astype(BHALF)
+    ends = []
+    for i in range(clips):
+        ends.append(k.lens[i] + (ends[-1] if i else 0))
+
+    def clip_of(frame):
+        total = (frame >= ends[0]).astype(jnp.int32)
+        for end in ends[1:]:
+            total = total + (frame >= end).astype(jnp.int32)
+        return total
+
+    span = every * HALF
+    left, right = iota((span, span), 0), iota((span, span), 1)
+    same = (left % HALF == right % HALF) & (clip_of(left // HALF) == clip_of(right // HALF))
+    near = jnp.abs(left // HALF - right // HALF) < MAXLEN
+    k.tmask[...] = jnp.where(same & near, 0.0, NEG)
+    onehot = []
+    for f in range(frames):
+        own = clip_of(jnp.full((1, model), s * frames + f, jnp.int32))
+        onehot.append([(own == i).astype(FLOAT) for i in range(clips)])
+    per_len = [1.0 / jnp.full((1, model), k.lens[i], jnp.int32).astype(FLOAT) for i in range(clips)]
+    cls32 = k.cls[...].astype(FLOAT)
+    cls_row = [sum(onehot[f][i] * cls32[i : i + 1] for i in range(clips)) for f in range(frames)]
+    tail = ROWS - patches
+
+    def set_tail(ref, f, first):
+        used_rows = sum(r.shape[0] for r in first)
+        fill = [jnp.zeros((tail - used_rows, model), FLOAT)] if used_rows < tail else []
+        ref[f * ROWS + patches : (f + 1) * ROWS, :] = jnp.concatenate(list(first) + fill, axis=0)
+
+    def eight(values):
+        missing = 8 - sum(v.shape[0] for v in values)
+        fill = [jnp.zeros((missing, model), FLOAT)] if missing else []
+        return jnp.concatenate(list(values) + fill, axis=0)
+
+    def norm(src, which, gain, shift, xhat, out):
+        def body(r):
+            v = src[r, :]
+            center = v - jnp.mean(v, axis=-1, keepdims=True)
+            invstd = lax.rsqrt(jnp.mean(center * center, axis=-1, keepdims=True) + EPS)
+            n = center * invstd
+            xhat[r, :] = n
+            k.inv[which, r, :] = jnp.broadcast_to(invstd, (BLOCK, 128))
+            out[r, :] = (n * gain + shift).astype(BHALF)
+
+        blocks(body, unroll=dims["unroll"])
+
+    l_tok.wait()
+    for f in range(frames):
+        k.x32[f * ROWS : f * ROWS + patches, :] = k.tok[f].astype(FLOAT)
+        set_tail(k.x32, f, [])
+    norm(k.x32, 0, t_gain, t_beta, k.xh_t, k.n_t)
+    l_ti.wait()
+
+    def to_slots(f, value, dst):
+        columns = value.shape[-1]
+        moved = dot_nn(k.sel[...], value).astype(BHALF)
+        dst[:, :, f] = moved.reshape(seq, 2, HALF, columns)
+
+    def from_slots(f, src):
+        columns = src.shape[-1]
+        return dot_nn(k.les[...], src[:, :, f].reshape(seq * SLOTS, columns))
+
+    for f in range(frames):
+        r = slice(f * ROWS, (f + 1) * ROWS)
+        qkv = (dot_nn(k.n_t[r, :], k.w_ti[...]) + t_qb).astype(BHALF)
+        to_slots(f, qkv, k.q_send)
+    l_to.wait()
+    l_so.wait()
+    pl.semaphore_wait(barrier, len(everyone))
+    mine = pl.ds(frames * s, frames)
+
+    def scatter(src, dst):
+        copies = [send(src.at[p], dst.at[:, mine], (p, h)) for p in peers]
+        dst[:, mine] = src[s]
+        return copies
+
+    def gather(src, dst):
+        copies = [send(src.at[:, pl.ds(frames * p, frames)], dst.at[s], (p, h)) for p in peers]
+        dst[s] = src[:, mine]
+        return copies
+
+    def arrived(copies):
+        for copy in copies:
+            copy.wait_recv()
+
+    q_copies = scatter(k.q_send, k.q_pos)
+
+    def share(ref):
+        return send(ref.at[0, c], ref.at[0, c], sister), send(ref.at[0, c], ref.at[1, c], across)
+
+    def pass_on(ref):
+        return send(ref.at[1, c], ref.at[1, c], sister)
+
+    w_to_near, w_to_far = share(k.w_to)
+    w_so_near, w_so_far = share(k.w_so)
+
+    l_og.wait()
+    cls_g = k.cls_grad[...].astype(FLOAT)
+    for f in range(frames):
+        k.gr32[f * ROWS : f * ROWS + patches, :] = k.out_grad[f].astype(FLOAT)
+        set_tail(k.gr32, f, [cls_g] if f == 0 else [])
+
+    def cast_rows(src, dst):
+        def body(r):
+            dst[r, :] = src[r, :].astype(BHALF)
+
+        blocks(body)
+
+    cast_rows(k.gr32, k.gr16)
+    l_dn.wait()
+    k.dact[...] = dot_nt(k.gr16[...], k.w_dn[...])
+    w_to_far.wait_recv()
+    w_to_last = pass_on(k.w_to)
+    w_so_far.wait_recv()
+    w_so_last = pass_on(k.w_so)
+
+    def attend(q, key, value, mask, p_ref):
+        scores = dot_nt(q, key) * scale + mask
+        e = jnp.exp(scores - jnp.max(scores, axis=-1, keepdims=True))
+        p = e * (1.0 / jnp.sum(e, axis=-1, keepdims=True))
+        p_ref[...] = p
+        return dot_nn(p.astype(BHALF), value).astype(BHALF)
+
+    def attend_back(q, key, value, grad, p_ref):
+        p = p_ref[...]
+        grad_p = p * dot_nt(grad, value)
+        grad_s = (grad_p - p * jnp.sum(grad_p, axis=-1, keepdims=True)).astype(BHALF)
+        grad_q = (dot_nn(grad_s, key) * scale).astype(BHALF)
+        grad_k = (dot_tn(grad_s, q) * scale).astype(BHALF)
+        grad_v = dot_tn(p.astype(BHALF), grad).astype(BHALF)
+        return grad_q, grad_k, grad_v
+
+    def head_of(value, part, j):
+        at = part * width + j * HEAD_DIM
+        return value[:, at : at + HEAD_DIM]
+
+    arrived(q_copies)
+    for b in range(2):
+        qkv = k.q_pos[b].reshape(span, 3 * width)
+        out = [
+            attend(head_of(qkv, 0, j), head_of(qkv, 1, j), head_of(qkv, 2, j), k.tmask[...], k.p_t.at[b * heads + j])
+            for j in range(heads)
+        ]
+        k.a_pos[b] = jnp.concatenate(out, axis=-1).reshape(every, HALF, width)
+    a_copies = gather(k.a_pos, k.a_recv)
+    arrived(a_copies)
+    for f in range(frames):
+        k.att_t[0, c, f * ROWS : (f + 1) * ROWS, :] = from_slots(f, k.a_recv).astype(BHALF)
+
+    def project(att, weight):
+        near, far = share(att)
+        near.wait_recv()
+        k.t32[...] = dot_nn(att[0, 0], weight[0, 0]) + dot_nn(att[0, 1], weight[0, 1])
+        far.wait_recv()
+        last = pass_on(att)
+        last.wait_recv()
+        k.u32[...] = dot_nn(att[1, 0], weight[1, 0]) + dot_nn(att[1, 1], weight[1, 1])
+
+    arrived([w_to_near, w_to_last])
+    project(k.att_t, k.w_to)
+
+    def mid_rows(r):
+        k.mid16[r, :] = (k.t32[r, :] + k.u32[r, :] + t_ob).astype(BHALF)
+
+    blocks(mid_rows)
+    l_tl.wait()
+    k.t32[...] = dot_nn(k.mid16[...], k.w_tl[...])
+
+    def add_res(r):
+        k.x32[r, :] = k.x32[r, :] + (k.t32[r, :] + t_lb).astype(BHALF).astype(FLOAT)
+
+    blocks(add_res)
+    for f in range(frames):
+        set_tail(k.x32, f, [cls_row[f]])
+
+    norm(k.x32, 1, s_gain, s_beta, k.xh_s, k.n_s)
+    l_si.wait()
+    k.sqkv[...] = (dot_nn(k.n_s[...], k.w_si[...]) + s_qb).astype(BHALF)
+    in_frame = jnp.where(iota((1, ROWS), 1) < patches + 1, 0.0, NEG)
+    for f in range(frames):
+        r = slice(f * ROWS, (f + 1) * ROWS)
+        qkv = k.sqkv[r, :]
+        out = [
+            attend(head_of(qkv, 0, j), head_of(qkv, 1, j), head_of(qkv, 2, j), in_frame, k.p_s.at[f * heads + j])
+            for j in range(heads)
+        ]
+        k.att_s[0, c, r, :] = jnp.concatenate(out, axis=-1)
+    arrived([w_so_near, w_so_last])
+    project(k.att_s, k.w_so)
+    at = [slice(f * ROWS + patches, f * ROWS + patches + 1) for f in range(frames)]
+    space_cls = [k.t32[r, :] + k.u32[r, :] + s_ob for r in at]
+    parts = [sum(onehot[f][i] * space_cls[f] for f in range(frames)) for i in range(clips)]
+    k.cls_send[...] = eight(parts)
+    cls_copies = [send(k.cls_send, k.cls_recv.at[s], (p, h)) for p in peers]
+    k.cls_recv[s] = k.cls_send[...]
+
+    def add_space(r):
+        k.x32[r, :] = k.x32[r, :] + (k.t32[r, :] + k.u32[r, :] + s_ob)
+
+    blocks(add_space)
+    arrived(cls_copies)
+    cls_sum = k.cls_recv[0]
+    for i in range(1, seq):
+        cls_sum = cls_sum + k.cls_recv[i]
+    cls_mid = [cls32[i : i + 1] + cls_sum[i : i + 1] * per_len[i] for i in range(clips)]
+    for f in range(frames):
+        set_tail(k.x32, f, cls_mid if f == 0 else [])
+
+    norm(k.x32, 2, m_gain, m_beta, k.xh_m, k.n_m)
+    l_up.wait()
+    k.t32[...] = dot_nn(k.n_m[...], k.w_up[...])
+    first_seq = jnp.where(s == 0, 1.0, 0.0)
+
+    def kept(r):
+        at = r.start + iota((BLOCK, 1), 0)
+        return jnp.where((at >= patches) & (at < ROWS), first_seq, 1.0)
+
+    def gelu_rows(r):
+        pre = k.t32[r, :] + m_ub
+        cdf = 0.5 * (1.0 + lax.erf(pre * 0.7071067811865476))
+        slope = cdf + pre * jnp.exp(-0.5 * pre * pre) * 0.3989422804014327
+        act = pre * cdf
+        grad = k.dact[r, :] * slope
+        keep = kept(r)
+        k.act[r, :] = act.astype(BHALF)
+        k.act_k[r, :] = (act * keep).astype(BHALF)
+        k.gpre[r, :] = grad.astype(BHALF)
+        k.gpre_k[r, :] = (grad * keep).astype(BHALF)
+
+    blocks(gelu_rows)
+
+    def sum_open(i, lhs, rhs, dot):
+        for b in range(2):
+            cut = slice(b * half, (b + 1) * half)
+            k.part[i, b] = dot(lhs[...], rhs[cut, :] if dot is dot_nt else rhs[:, cut]).astype(BHALF)
+        return send(k.part.at[i, other_c], k.pair.at[i], sister)
+
+    def sum_across(i, copy):
+        copy.wait_recv()
+        k.part[i, c] = (k.part[i, c].astype(FLOAT) + k.pair[i].astype(FLOAT)).astype(BHALF)
+        return send(k.part.at[i, c], k.other.at[i], across)
+
+    def sum_close(i, copy):
+        copy.wait_recv()
+        k.total[i, c] = (k.part[i, c].astype(FLOAT) + k.other[i].astype(FLOAT)).astype(BHALF)
+        return send(k.total.at[i, c], k.total.at[i, c], sister)
+
+    def sum_rows(i, r):
+        return jnp.concatenate([k.total[i, 0, r, :], k.total[i, 1, r, :]], axis=-1).astype(FLOAT)
+
+    def grad_open(name, lhs, rhs):
+        g, got = getattr(k, "g_" + name), getattr(k, "y_" + name)
+        g[...] = dot_tn(lhs, rhs).astype(BHALF).reshape(g.shape)
+        return name, send(g.at[:, 1 - y], got, y_peer)
+
+    def grad_along(job):
+        name, copy = job
+        g, got, last = [getattr(k, kind + name) for kind in ("g_", "y_", "z_")]
+        copy.wait_recv()
+        g[:, y] = (g[:, y].astype(FLOAT) + got[...].astype(FLOAT)).astype(BHALF)
+        last[z] = g[z, y]
+        return name, [send(g.at[p, y], last.at[z], (p * 2 + y, h)) for p in z_peers]
+
+    def grad_close(job):
+        name, copies = job
+        last, out = getattr(k, "z_" + name), getattr(k, "o_" + name)
+        arrived(copies)
+        out[...] = sum(last[i].astype(FLOAT) for i in range(zs))
+
+    def vectors_send(which, values):
+        value = eight(values)
+        k.v_send[which] = value
+        k.v_recv[which, s] = value
+        return [send(k.v_send.at[which], k.v_recv.at[which, s], (p, h)) for p in peers]
+
+    def vectors_close(which, copies):
+        arrived(copies)
+        value = k.v_recv[which, 0]
+        for i in range(1, seq):
+            value = value + k.v_recv[which, i]
+        return value
+
+    ones = jnp.ones((8, rows), BHALF)
+    at = iota((8, rows), 1)
+    ones_kept = jnp.where((at >= patches) & (at < ROWS), first_seq, 1.0).astype(BHALF)
+
+    def col_sums(ref, weights=None):
+        out = dot_nn(ones if weights is None else weights, ref[...])[0:1]
+        if out.shape[1] < model:
+            out = jnp.concatenate([out, jnp.zeros((1, model - out.shape[1]), FLOAT)], axis=-1)
+        return out
+
+    def norm_back(i, which, gain, xhat, keep, use):
+        def body(r, sums):
+            g = sum_rows(i, r)
+            n = xhat[r, :]
+            gh = g * gain
+            m1 = jnp.mean(gh, axis=-1, keepdims=True)
+            m2 = jnp.mean(gh * n, axis=-1, keepdims=True)
+            use(r, k.inv[which, r, 0:1] * (gh - m1 - n * m2))
+            w = g * kept(r) if keep else g
+            fold = lambda v: jnp.sum(v.reshape(BLOCK // 8, 8, model), axis=0)
+            return sums[0] + fold(w * n), sums[1] + fold(w)
+
+        zero = jnp.zeros((8, model), FLOAT)
+        sums = (zero, zero)
+        if dims["unroll"]:
+            for b in range(rows // BLOCK):
+                sums = body(pl.ds(b * BLOCK, BLOCK), sums)
+        else:
+            sums = lax.fori_loop(
+                0, rows // BLOCK, lambda b, v: body(pl.ds(pl.multiple_of(b * BLOCK, BLOCK), BLOCK), v), sums
+            )
+        return [jnp.sum(v, axis=0, keepdims=True) for v in sums]
+
+    m_sum = sum_open(0, k.gpre, k.w_up, dot_nt)
+    j_dn = grad_open("dn", k.gr16[...], k.act_k[...])
+    m_sum = sum_across(0, m_sum)
+    j_up = grad_open("up", k.n_m[...], k.gpre_k[...])
+    o_sum = sum_open(1, k.act, k.w_dn, dot_nn)
+    j_dn = grad_along(j_dn)
+    o_sum = sum_across(1, o_sum)
+    ub_grad, db_grad = col_sums(k.gpre_k), col_sums(k.gr16, ones_kept)
+    j_up = grad_along(j_up)
+    last = sum_close(0, m_sum)
+    last.wait_recv()
+
+    def use_m(r, dx):
+        k.gr32[r, :] = k.gr32[r, :] + dx
+
+    sums = norm_back(0, 2, m_gain, k.xh_m, True, use_m)
+    v_m = vectors_send(0, [sums[0], sums[1], ub_grad, db_grad])
+    grad_cls_mid = k.gr32[patches : patches + clips, :]
+    k.gcm[...] = eight([grad_cls_mid])
+    for f in range(frames):
+        shared = sum(onehot[f][i] * (grad_cls_mid[i : i + 1] * per_len[i]) for i in range(clips))
+        set_tail(k.gr32, f, [shared])
+    cast_rows(k.gr32, k.gss)
+    for f in range(frames):
+        set_tail(k.gr32, f, [])
+
+    k.gatt[...] = dot_nt(k.gss[...], k.w_so[0, c]).astype(BHALF)
+    for f in range(frames):
+        r = slice(f * ROWS, (f + 1) * ROWS)
+        qkv, grad = k.sqkv[r, :], k.gatt[r, :]
+        out = [
+            attend_back(*[head_of(qkv, i, j) for i in range(3)], head_of(grad, 0, j), k.p_s.at[f * heads + j])
+            for j in range(heads)
+        ]
+        k.dsq[r, :] = jnp.concatenate([out[j][i] for i in range(3) for j in range(heads)], axis=-1)
+    s_sum = sum_open(2, k.dsq, k.w_si, dot_nt)
+    j_si = grad_open("si", k.n_s[...], k.dsq[...])
+    s_sum = sum_across(2, s_sum)
+    last = sum_close(1, o_sum)
+    j_so = grad_open("so", k.gss[...], k.att_s[0, c])
+    j_si = grad_along(j_si)
+    last.wait_recv()
+
+    def out_rows(r):
+        k.t32[r, :] = k.x32[r, :] + sum_rows(1, r) + m_db
+
+    blocks(out_rows)
+    for f in range(frames):
+        k.o_blk[f] = k.t32[f * ROWS : f * ROWS + patches, :].astype(BHALF)
+    k.o_cls[...] = k.t32[patches : patches + clips, :].astype(BHALF)
+    s_rows = [col_sums(k.gss), col_sums(k.dsq)]
+    j_so = grad_along(j_so)
+    last = sum_close(2, s_sum)
+    last.wait_recv()
+    sums = norm_back(2, 1, s_gain, k.xh_s, False, use_m)
+    cls_in = [k.gr32[f * ROWS + patches : f * ROWS + patches + 1, :] for f in range(frames)]
+    cls_parts = [sum(onehot[f][i] * cls_in[f] for f in range(frames)) for i in range(clips)]
+    for f in range(frames):
+        set_tail(k.gr32, f, [])
+    v_s = vectors_send(1, [sums[0], sums[1]] + s_rows + cls_parts)
+    cast_rows(k.gr32, k.gtr)
+
+    k.gtm[...] = dot_nt(k.gtr[...], k.w_tl[...]).astype(BHALF)
+    k.gatt[...] = dot_nt(k.gtm[...], k.w_to[0, c]).astype(BHALF)
+    for f in range(frames):
+        to_slots(f, k.gatt[f * ROWS : (f + 1) * ROWS, :], k.g_send)
+    g_copies = scatter(k.g_send, k.g_pos)
+    pick = (iota((model, width), 0) == h * width + iota((model, width), 1)).astype(FLOAT).astype(BHALF)
+    j_tl = grad_open("tl", k.mid16[...], dot_nn(k.gtr[...], pick).astype(BHALF))
+    j_to = grad_open("to", k.gtm[...], k.att_t[0, c])
+    t_rows = [col_sums(k.gtm), col_sums(k.gtr)]
+    arrived(g_copies)
+    for b in range(2):
+        qkv, grad = k.q_pos[b].reshape(span, 3 * width), k.g_pos[b].reshape(span, width)
+        out = [
+            attend_back(*[head_of(qkv, i, j) for i in range(3)], head_of(grad, 0, j), k.p_t.at[b * heads + j])
+            for j in range(heads)
+        ]
+        value = jnp.concatenate([out[j][i] for i in range(3) for j in range(heads)], axis=-1)
+        k.d_pos[b] = value.reshape(every, HALF, 3 * width)
+    d_copies = gather(k.d_pos, k.d_recv)
+    j_tl = grad_along(j_tl)
+    j_to = grad_along(j_to)
+    grad_close(j_dn)
+    grad_close(j_up)
+    m_vec = vectors_close(0, v_m)
+    s_vec = vectors_close(1, v_s)
+    arrived(d_copies)
+    for f in range(frames):
+        k.dtq[f * ROWS : (f + 1) * ROWS, :] = from_slots(f, k.d_recv).astype(BHALF)
+    t_sum = sum_open(3, k.dtq, k.w_ti, dot_nt)
+    j_ti = grad_open("ti", k.n_t[...], k.dtq[...])
+    t_sum = sum_across(3, t_sum)
+    pair_row = col_sums(k.dtq)
+    grad_close(j_si)
+    grad_close(j_so)
+    j_ti = grad_along(j_ti)
+    grad_close(j_tl)
+    grad_close(j_to)
+    last = sum_close(3, t_sum)
+    last.wait_recv()
+
+    def use_t(r, dx):
+        k.t32[r, :] = k.gr32[r, :] + dx.astype(BHALF).astype(FLOAT)
+
+    sums = norm_back(3, 0, t_gain, k.xh_t, False, use_t)
+    v_t = vectors_send(2, [sums[0], sums[1], t_rows[0], pair_row, t_rows[1]])
+    for f in range(frames):
+        k.o_tok[f] = k.t32[f * ROWS : f * ROWS + patches, :].astype(BHALF)
+    k.o_vec[0:8, :] = m_vec
+    k.o_vec[8:16, :] = s_vec + jnp.concatenate([jnp.zeros((4, model), FLOAT), k.gcm[0:4, :]], axis=0)
+    k.o_vec[16:24, :] = vectors_close(2, v_t)
+    grad_close(j_ti)
+    for copy in unsent:
+        copy.wait_send()
+
+
+def finish_kernel(dims, vec, g_dn, g_up, g_si, g_so, g_tl, g_to, g_ti, *outs):
+    width, model, seq = dims["width"], dims["model"], dims["seq"]
+    share, clips = model // seq, dims["clips"]
+    cls, tg, tb, ti, tp, to, tob, tl, tlb, sg, sb, si, sp, so, sob, mg, mb, up, ub, dn, db = outs
+    s = lax.axis_index("seq")
+    v = vec[...]
+    mine = pltpu.roll(v, (model - share * s) % model, 1)[:, :share]
+    mg[...], mb[...], ub[...], db[...] = mine[0:1], v[1:2], v[2:3], v[3:4]
+    sg[...], sb[...], sob[...] = mine[8:9], v[9:10], v[10:11]
+    tg[...], tb[...], tob[...], tlb[...] = mine[16:17], v[17:18], v[18:19], v[20:21]
+    cls[...] = mine[12 : 12 + clips]
+    for out, row in ((sp, 11), (tp, 19)):
+        out[0:1, :] = v[row : row + 1, :width]
+        out[1:2, :] = v[row : row + 1, 2 * width : 3 * width]
+    for out, g in ((si, g_si), (ti, g_ti)):
+        for i in range(3):
+            out[:, i, :] = g[:, i * width : (i + 1) * width]
+    tl[...] = g_tl[...]
+    up[...] = g_up[...]
+    to[...] = g_to[...].T
+    so[...] = g_so[...].T
+    dn[...] = g_dn[...].T
+
+
+def fused_body(
+    tokens,
+    cls_tokens,
+    clip_lengths,
+    time_gain,
+    time_beta,
+    time_proj_in,
+    time_qv_bias,
+    time_proj_out,
+    time_out_bias,
+    time_linear,
+    time_linear_bias,
+    space_gain,
+    space_beta,
+    space_proj_in,
+    space_qv_bias,
+    space_proj_out,
+    space_out_bias,
+    mlp_gain,
+    mlp_beta,
+    mlp_up,
+    mlp_up_bias,
+    mlp_down,
+    mlp_down_bias,
+    out_grad,
+    cls_grad,
+):
+    frames, patches, model = tokens.shape
+    seq = lax.axis_size("seq")
+    width, hidden, clips = time_proj_in.shape[2], mlp_up.shape[1], clip_lengths.shape[0]
+    dims = dict(
+        frames=frames,
+        patches=patches,
+        model=model,
+        seq=seq,
+        width=width,
+        hidden=hidden,
+        clips=clips,
+        pos=-(-patches // seq),
+        unroll=False,
+    )
+
+    def wide(v):
+        return jnp.pad(v, (0, model - v.shape[0]))
+
+    vec = jnp.stack(
+        [
+            time_gain,
+            time_beta,
+            time_out_bias,
+            time_linear_bias,
+            space_gain,
+            space_beta,
+            space_out_bias,
+            mlp_gain,
+            mlp_beta,
+            mlp_down_bias,
+            mlp_up_bias,
+            wide(qkv_shift(time_qv_bias)),
+            wide(qkv_shift(space_qv_bias)),
+        ]
+    )
+    scratch = scratch_shapes(dims)
+    grads = grad_columns(dims)
+    share = model // seq
+    shape = jax.ShapeDtypeStruct
+    vmem, anywhere = pl.BlockSpec(memory_space=pltpu.VMEM), pl.BlockSpec(memory_space=pl.ANY)
+    outs = [
+        shape(tokens.shape, BHALF),
+        shape(cls_tokens.shape, BHALF),
+        shape(tokens.shape, BHALF),
+        shape((24, model), FLOAT),
+    ] + [shape((share, columns), FLOAT) for _, columns in grads]
+    names = list(INPUTS) + list(OUTPUTS) + ["o_" + name for name, _ in grads] + list(scratch)
+    results = pl.pallas_call(
+        functools.partial(layer_kernel, dims, names),
+        out_shape=outs,
+        in_specs=[pl.BlockSpec(memory_space=pltpu.SMEM)] + [vmem] * 3 + [anywhere] * 9,
+        out_specs=[vmem] * len(outs),
+        scratch_shapes=list(scratch.values()),
+        compiler_params=pltpu.CompilerParams(
+            collective_id=0, has_side_effects=True, vmem_limit_bytes=62 * 1024 * 1024
+        ),
+        name="layer",
+    )(
+        clip_lengths,
+        cls_tokens,
+        cls_grad,
+        vec,
+        tokens,
+        out_grad,
+        time_proj_in.reshape(model, 3 * width),
+        time_proj_out,
+        time_linear,
+        space_proj_in.reshape(model, 3 * width),
+        space_proj_out,
+        mlp_up,
+        mlp_down,
+    )
+    block_out, cls_out, tokens_grad = results[:3]
+    row, gain = shape((1, model), FLOAT), shape((1, share), FLOAT)
+    proj, pair = shape((share, 3, width), FLOAT), shape((2, width), FLOAT)
+    out_shape = [
+        shape((clips, share), FLOAT),
+        gain,
+        row,
+        proj,
+        pair,
+        shape((width, share), FLOAT),
+        row,
+        shape((share, width), FLOAT),
+        row,
+        gain,
+        row,
+        proj,
+        pair,
+        shape((width, share), FLOAT),
+        row,
+        gain,
+        row,
+        shape((share, hidden), FLOAT),
+        shape((1, hidden), FLOAT),
+        shape((hidden, share), FLOAT),
+        row,
+    ]
+    last = pl.pallas_call(
+        functools.partial(finish_kernel, dims),
+        out_shape=out_shape,
+        in_specs=[vmem] * 8,
+        out_specs=[vmem] * len(out_shape),
+        compiler_params=pltpu.CompilerParams(vmem_limit_bytes=32 * 1024 * 1024),
+        name="finish",
+    )(*results[3:])
+    last = [v.reshape(-1) if v.shape[0] == 1 else v for v in last]
+    return (block_out, cls_out, tokens_grad, *last)
+
+
 def solution(mesh):
     placed = (
         P("seq", None, None),
@@ -488,8 +1287,9 @@
         P("seq", None, None),
         P(),
     )
+    fused = mesh.shape["seq"] == 8 and mesh.shape["head"] == 4
     return jax.shard_map(
-        body,
+        fused_body if fused else body,
         mesh=mesh,
         in_specs=placed,
         out_specs=(

time: 1070 us -> 224 us (0.21)
  waiting for transfers between devices: 655 us -> 0 us
  Pallas kernels: 0 us -> 196 us
  local copies, waits for them, and re-layouts: 130 us -> 22.3 us
  blocking collectives: 94.5 us -> 0 us
  matrix products: 73.9 us -> 0 us
  other arithmetic: 73.8 us -> 4.91 us
  starting transfers between devices: 23.8 us -> 0 us
  between operations: 16.2 us -> 0.81 us
    reduce_scatter x5 -> x0, waiting for transfers between devices: 348 us -> none  [the longest x1 72.2 us: body(): lax.psum_scatter(up_grad, 'seq', scatter_dimension=0, tiled=True)]
    pallas_call x0 -> x2, Pallas kernels: none -> 196 us  [the longest x1 195 us: fused_body(): pl.pallas_call(functools.partial(layer_kernel, dims, names), out_shape=ou...]
    unnamed x16 -> x0, waiting for transfers between devices: 140 us -> none
    psum x5 -> x0, waiting for transfers between devices: 119 us -> none  [the longest x1 32 us: body(): lax.psum(matmul_plain(time_att, time_proj_out).astype(jnp.bfloat16), 'head')]
    dot_general x32 -> x0, matrix products: 67 us -> none  [the longest x5 16.5 us: matmul_tn(): lax.dot_general(left, right, (((0,), (0,)), ((), ())), preferred_element_...]
    all_to_all x4 -> x0, waiting for transfers between devices: 48.5 us -> none  [the longest x2 28.3 us: to_positions(): lax.all_to_all(padded.reshape(frames_dev, seq_count, pos_dev, columns), '...]
    psum x1 -> x0, blocking collectives: 37.1 us -> none  [body(): lax.psum(cls_part, 'seq') / lengths[:, None]]
    unnamed x1 -> x0, blocking collectives: 36.8 us -> none
  transfers between devices with their start and end apart: 17 -> 0, of which waited for: 15 -> 0; matrix products, arithmetic and copies ran while one was open for 7% -> 0% of each run, Pallas kernels for 0% -> 0%
where the time goes in v1:
time: 224 us
  Pallas kernels  196 us (88%)
  local copies, waits for them, and re-layouts  22.3 us (10%)
  other arithmetic  4.91 us (2%)
    pallas_call x1, Pallas kernels, fused_body(): pl.pallas_call(functools.partial(layer_kernel, dims, names), out_shape=ou...  195 us
    unnamed x34, local copies, waits for them, and re-layouts  9.75 us
    another operation x14, local copies, waits for them, and re-layouts, fused_body(): jnp.stack([time_gain, time_beta, time_out_bias, time_linear_bias, space_g...  8.92 us
    pallas_call x8, other arithmetic, fused_body(): pl.pallas_call(functools.partial(finish_kernel, dims), out_shape=out_shap...  4.84 us

profile of v1, /device:TPU:0, one launch (start us, length us, event | category | flops | bytes accessed | tf_op | source)
XLA Modules:
  0.0 223.8 jit_solution(9417839702499245271)
XLA Ops:
  0.7 0.0 copy-start.11
  0.7 0.1 pad.13.clone
  0.7 0.7 stack.48
  1.5 0.7 stack.49
  2.2 0.7 stack.50
  2.9 0.7 stack.51
  3.5 0.7 stack.52
  4.2 0.7 stack.53
  4.9 0.7 stack.54
  5.6 0.7 stack.55
  6.3 0.7 stack.56
  7.0 0.7 stack.58
  7.7 0.7 stack.57
  8.4 0.8 fusion
  9.1 0.1 pad_maximum_fusion.1
  9.2 0.1 reshape.94
  9.3 0.1 reshape.93
  9.4 1.3 stack.63.refs_3_
  10.7 0.0 copy-start.8
  10.7 2.0 copy.58.refs_4_
  12.7 0.0 copy-done.11
  12.7 0.9 copy.59.refs_5_
  13.6 0.0 copy-done.8
  13.6 0.0 copy-start.9
  13.6 1.3 copy.60.refs_6_
  14.9 0.0 copy-done.9
  14.9 1.3 copy.61.refs_9_
  16.3 194.5 %layer.1 = (bf16[2,196,768]{2,1,0:T(8,128)(2,1)}, bf16[4,768]{1,0:T(4,128)(2,1)}, bf16[2,196,768]{2,1,0:T(8,128)(2,1)}, f32[24,768]{1,0:T(8,128)}, f32[96,768]{1...) custom-call(s32[4]{0:T(128)} %refs_0_.1, ...), custom_call_target="tpu_custom_call" | custom-call | tf_op jit(solution)/shard_map/layer/pallas_call | solution.py:1199
  210.8 0.0 copy-start.10
  210.8 0.0 copy-start
  210.8 0.0 copy-start.1
  210.8 0.0 copy-start.2
  210.8 0.0 copy-start.3
  210.8 0.0 copy-start.4
  210.8 0.0 copy-start.5
  210.8 0.0 copy-start.6
  210.9 0.0 copy-start.7
  210.9 2.5 %copy.62 = bf16[2,196,768]{2,0,1:T(2,128)(2,1)} copy(bf16[2,196,768]{2,1,0:T(8,128)(2,1)} %get-tuple-element.112) | data formatting | bytes 1204224
  213.4 0.0 copy-done.10
  213.4 1.3 copy.63
  214.6 0.0 copy-done
  214.6 0.0 copy-done.1
  214.6 0.0 copy-done.2
  214.6 0.0 copy-done.3
  214.7 0.0 copy-done.4
  214.7 0.0 copy-done.5
  214.7 0.0 copy-done.6
  214.7 0.0 copy-done.7
  214.7 1.2 finish.1
  215.9 0.0 copy-start.12
  215.9 0.6 reduce
  216.5 0.6 reduce.1
  217.1 0.6 reduce.2
  217.7 0.6 reduce.3
  218.3 0.6 reduce.4
  218.9 0.6 reduce.5
  219.6 0.6 reduce.6
  220.2 0.6 reduce.7
  220.8 0.8 copy.64
  221.5 0.8 copy.65
  222.3 0.9 copy.66
  223.2 0.0 copy-done.12
  223.2 0.6 copy.68
  (4 shorter events, 0.0 us)
Async XLA Ops:
  0.7 12.1 %copy-start.11 = (bf16[2,196,768]{2,0,1:T(2,128)(2,1)S(1)}, bf16[2,196,768]{2,0,1:T(2,128)(2,1)}, u32[]{:S(2)}) copy-start(bf16[2,196,768]{2,0,1:T(2,128)(2,1)} %param.48) | copy-start | bytes 1806340
  10.7 2.9 %copy-start.8 = (bf16[768,3,192]{0,2,1:T(8,128)(2,1)S(1)}, bf16[768,3,192]{0,2,1:T(8,128)(2,1)}, u32[]{:S(2)}) copy-start(bf16[768,3,192]{0,2,1:T(8,128)(2,1)} %param.30) | copy-start | bytes 2654212
  13.6 1.3 copy-start.9
  210.8 2.6 %copy-start.10 = (bf16[2,196,768]{2,1,0:T(8,128)(2,1)S(1)}, bf16[2,196,768]{2,1,0:T(8,128)(2,1)}, u32[]{:S(2)}) copy-start(bf16[2,196,768]{2,1,0:T(8,128)(2,1)} %get-tuple-element.114) | copy-start | bytes 1806340
  210.8 3.9 %copy-start = (f32[96,768]{1,0:T(8,128)S(1)}, f32[96,768]{1,0:T(8,128)}, u32[]{:S(2)}) copy-start(f32[96,768]{1,0:T(8,128)} %get-tuple-element.60.g_dn) | copy-start | bytes 884740
  210.8 3.8 %copy-start.1 = (f32[96,768]{1,0:T(8,128)S(1)}, f32[96,768]{1,0:T(8,128)}, u32[]{:S(2)}) copy-start(f32[96,768]{1,0:T(8,128)} %get-tuple-element.61.g_up) | copy-start | bytes 884740
  210.8 3.8 %copy-start.2 = (f32[96,576]{1,0:T(8,128)S(1)}, f32[96,576]{1,0:T(8,128)}, u32[]{:S(2)}) copy-start(f32[96,576]{1,0:T(8,128)} %get-tuple-element.62.g_si) | copy-start | bytes 663556
  210.8 3.8 %copy-start.3 = (f32[96,576]{1,0:T(8,128)S(1)}, f32[96,576]{1,0:T(8,128)}, u32[]{:S(2)}) copy-start(f32[96,576]{1,0:T(8,128)} %get-tuple-element.66.g_ti) | copy-start | bytes 663556
  210.8 3.8 %copy-start.4 = (f32[96,192]{1,0:T(8,128)S(1)}, f32[96,192]{1,0:T(8,128)}, u32[]{:S(2)}) copy-start(f32[96,192]{1,0:T(8,128)} %get-tuple-element.63.g_so) | copy-start | bytes 221188
  210.8 3.8 %copy-start.5 = (f32[96,192]{1,0:T(8,128)S(1)}, f32[96,192]{1,0:T(8,128)}, u32[]{:S(2)}) copy-start(f32[96,192]{1,0:T(8,128)} %get-tuple-element.64.g_tl) | copy-start | bytes 221188
  210.8 3.8 %copy-start.6 = (f32[96,192]{1,0:T(8,128)S(1)}, f32[96,192]{1,0:T(8,128)}, u32[]{:S(2)}) copy-start(f32[96,192]{1,0:T(8,128)} %get-tuple-element.65.g_to) | copy-start | bytes 221188
  210.9 3.8 %copy-start.7 = (f32[24,768]{1,0:T(8,128)S(1)}, f32[24,768]{1,0:T(8,128)}, u32[]{:S(2)}) copy-start(f32[24,768]{1,0:T(8,128)} %get-tuple-element.59.vec) | copy-start | bytes 221188
  215.9 7.3 %copy-start.12 = (bf16[4,768]{1,0:T(4,128)(2,1)S(1)}, bf16[4,768]{1,0:T(4,128)(2,1)}, u32[]{:S(2)}) copy-start(bf16[4,768]{1,0:T(4,128)(2,1)} %get-tuple-element.169) | copy-start | bytes 18436

commit v2 on v1

--- a/solution.py
+++ b/solution.py
@@ -495,10 +495,10 @@
     half, low = model // 2, BHALF
     vm = pltpu.VMEM
     shapes = dict(
-        tok=vm((frames, dims["patches"], model), low),
-        out_grad=vm((frames, dims["patches"], model), low),
-        w_ti=vm((model, 3 * width), low),
-        w_si=vm((model, 3 * width), low),
+        tok=vm((dims["patches"], frames, model), low),
+        out_grad=vm((dims["patches"], frames, model), low),
+        w_ti=vm((3 * width, model), low),
+        w_si=vm((3 * width, model), low),
         w_tl=vm((model, model), low),
         w_up=vm((model, hidden), low),
         w_dn=vm((hidden, model), low),
@@ -534,14 +534,14 @@
         tmask=vm((every * HALF, every * HALF), FLOAT),
         p_t=vm((2 * heads, every * HALF, every * HALF), FLOAT),
         p_s=vm((frames * heads, ROWS, ROWS), FLOAT),
-        q_send=vm((seq, 2, frames, HALF, 3 * width), low),
+        q_send=vm((frames, seq, 2, HALF, 3 * width), low),
         q_pos=vm((2, every, HALF, 3 * width), low),
         a_pos=vm((2, every, HALF, width), low),
-        a_recv=vm((seq, 2, frames, HALF, width), low),
-        g_send=vm((seq, 2, frames, HALF, width), low),
+        a_recv=vm((2, seq, frames, HALF, width), low),
+        g_send=vm((frames, seq, 2, HALF, width), low),
         g_pos=vm((2, every, HALF, width), low),
         d_pos=vm((2, every, HALF, 3 * width), low),
-        d_recv=vm((seq, 2, frames, HALF, 3 * width), low),
+        d_recv=vm((2, seq, frames, HALF, 3 * width), low),
         att_t=vm((2, 2, rows, width), low),
         att_s=vm((2, 2, rows, width), low),
         part=vm((4, 2, rows, half), low),
@@ -553,14 +553,19 @@
         gcm=vm((8, model), FLOAT),
         v_send=vm((3, 8, model), FLOAT),
         v_recv=vm((3, seq, 8, model), FLOAT),
+        v_head=vm((4, 8, model), FLOAT),
     )
     for name, columns in grad_columns(dims):
         shapes["g_" + name] = vm((seq // 2, 2, model // seq, columns), low)
         shapes["y_" + name] = vm((seq // 2, model // seq, columns), low)
         shapes["z_" + name] = vm((seq // 2, model // seq, columns), low)
-    shapes["load"] = pltpu.SemaphoreType.DMA((16,))
-    shapes["sent"] = pltpu.SemaphoreType.DMA((160,))
-    shapes["got"] = pltpu.SemaphoreType.DMA((160,))
+    for name in VECTORS:
+        shapes[name] = vm((hidden if name == "m_ub" else model,), FLOAT)
+    for name in PAIRS:
+        shapes[name] = vm((2, width), FLOAT)
+    shapes["load"] = pltpu.SemaphoreType.DMA((32,))
+    shapes["sent"] = pltpu.SemaphoreType.DMA((240,))
+    shapes["got"] = pltpu.SemaphoreType.DMA((240,))
     return shapes
 
 
@@ -577,7 +582,10 @@
     )
 
 
-INPUTS = ("lens", "cls", "cls_grad", "vec", "h_tok", "h_og", "h_ti", "h_to", "h_tl", "h_si", "h_so", "h_up", "h_dn")
+VECTORS = ("t_gain", "t_beta", "t_ob", "t_lb", "s_gain", "s_beta", "s_ob", "m_gain", "m_beta", "m_db", "m_ub")
+PAIRS = ("t_qv", "s_qv")
+MATRICES = ("tok", "out_grad", "w_ti", "w_to", "w_tl", "w_si", "w_so", "w_up", "w_dn")
+INPUTS = ("lens", "cls", "cls_grad") + tuple("h_" + name for name in VECTORS + PAIRS + MATRICES)
 OUTPUTS = ("o_blk", "o_cls", "o_tok", "o_vec")
 
 
@@ -598,7 +606,7 @@
     z, y = s // 2, s % 2
     x, c = h // 2, h % 2
     other_c = 1 - c
-    sister, across = (s, x * 2 + other_c), (s, (1 - x) * 2 + c)
+    sister, across, diagonal = (s, x * 2 + other_c), (s, (1 - x) * 2 + c), (s, (1 - x) * 2 + other_c)
     y_peer = (z * 2 + 1 - y, h)
     z_peers = [((z + i) % zs) for i in range(1, zs)]
     peers = [((z + i) % zs) * 2 + (y + j) % 2 for i in range(zs) for j in range(2) if i or j]
@@ -640,32 +648,38 @@
 
             lax.fori_loop(0, rows // BLOCK, step, 0)
 
-    l_tok = load(k.h_tok, k.tok)
-    l_ti = load(k.h_ti, k.w_ti)
-    l_to = load(k.h_to, k.w_to.at[0, c])
-    l_so = load(k.h_so, k.w_so.at[0, c])
-    l_og = load(k.h_og, k.out_grad)
-    l_dn = load(k.h_dn, k.w_dn)
-    l_tl = load(k.h_tl, k.w_tl)
-    l_si = load(k.h_si, k.w_si)
-    l_up = load(k.h_up, k.w_up)
+    places = {"w_to": k.w_to.at[0, c], "w_so": k.w_so.at[0, c]}
+    order = ("tok", "t_gain", "t_beta", "w_ti", "t_qv", "w_to", "w_so", "out_grad", "w_dn") + VECTORS[2:] + ("s_qv", "w_tl", "w_si", "w_up")
+    loading = {name: load(getattr(k, "h_" + name), places.get(name, getattr(k, name))) for name in order}
+
+    def need(*wanted):
+        for name in wanted:
+            loading.pop(name).wait()
+
     barrier = pltpu.get_barrier_semaphore()
-    everyone = [(p, h) for p in peers] + [sister, across]
+    everyone = [(p, h) for p in peers] + [sister, across, diagonal]
     for device in everyone:
         pl.semaphore_signal(barrier, inc=1, device_id=device, device_id_type=MESH)
 
-    def vec(i):
-        return k.vec[i : i + 1, :]
-
-    t_gain, t_beta, t_ob, t_lb, s_gain, s_beta, s_ob, m_gain, m_beta, m_db, m_ub = [vec(i) for i in range(11)]
-    t_qb, s_qb = vec(11)[:, : 3 * width], vec(12)[:, : 3 * width]
-
-    slot, row = iota((seq * SLOTS, ROWS), 0), iota((seq * SLOTS, ROWS), 1)
-    place = (slot // SLOTS) * pos + slot % SLOTS
-    k.sel[...] = jnp.where((place == row) & (slot % SLOTS < pos) & (row < patches), 1.0, 0.0).astype(BHALF)
-    row, slot = iota((ROWS, seq * SLOTS), 0), iota((ROWS, seq * SLOTS), 1)
-    place = (slot // SLOTS) * pos + slot % SLOTS
-    k.les[...] = jnp.where((place == row) & (slot % SLOTS < pos) & (row < patches), 1.0, 0.0).astype(BHALF)
+    def vec(name):
+        if name in loading:
+            need(name)
+        return getattr(k, name)[...].reshape(1, -1)
+
+    def qkv_row(name):
+        need(name)
+        pair = getattr(k, name)
+        return jnp.concatenate([pair[0:1, :], jnp.zeros((1, width), FLOAT), pair[1:2, :]], axis=-1)
+
+    def chosen(slot, row, outer):
+        if outer:
+            device, place = slot // SLOTS, slot % SLOTS
+        else:
+            device, place = slot // HALF % seq, slot // (HALF * seq) * HALF + slot % HALF
+        hit = (device * pos + place == row) & (place < pos) & (row < patches)
+        return jnp.where(hit, 1.0, 0.0).astype(BHALF)
+
+    k.sel[...] = chosen(iota((seq * SLOTS, ROWS), 0), iota((seq * SLOTS, ROWS), 1), True)
     ends = []
     for i in range(clips):
         ends.append(k.lens[i] + (ends[-1] if i else 0))
@@ -676,11 +690,6 @@
             total = total + (frame >= end).astype(jnp.int32)
         return total
 
-    span = every * HALF
-    left, right = iota((span, span), 0), iota((span, span), 1)
-    same = (left % HALF == right % HALF) & (clip_of(left // HALF) == clip_of(right // HALF))
-    near = jnp.abs(left // HALF - right // HALF) < MAXLEN
-    k.tmask[...] = jnp.where(same & near, 0.0, NEG)
     onehot = []
     for f in range(frames):
         own = clip_of(jnp.full((1, model), s * frames + f, jnp.int32))
@@ -700,58 +709,56 @@
         fill = [jnp.zeros((missing, model), FLOAT)] if missing else []
         return jnp.concatenate(list(values) + fill, axis=0)
 
+    def norm_rows(src, which, gain, shift, xhat, out, r):
+        v = src[r, :]
+        center = v - jnp.mean(v, axis=-1, keepdims=True)
+        invstd = lax.rsqrt(jnp.mean(center * center, axis=-1, keepdims=True) + EPS)
+        n = center * invstd
+        xhat[r, :] = n
+        k.inv[which, r, :] = jnp.broadcast_to(invstd, (v.shape[0], 128))
+        out[r, :] = (n * gain + shift).astype(BHALF)
+
     def norm(src, which, gain, shift, xhat, out):
-        def body(r):
-            v = src[r, :]
-            center = v - jnp.mean(v, axis=-1, keepdims=True)
-            invstd = lax.rsqrt(jnp.mean(center * center, axis=-1, keepdims=True) + EPS)
-            n = center * invstd
-            xhat[r, :] = n
-            k.inv[which, r, :] = jnp.broadcast_to(invstd, (BLOCK, 128))
-            out[r, :] = (n * gain + shift).astype(BHALF)
-
-        blocks(body, unroll=dims["unroll"])
-
-    l_tok.wait()
-    for f in range(frames):
-        k.x32[f * ROWS : f * ROWS + patches, :] = k.tok[f].astype(FLOAT)
+        blocks(lambda r: norm_rows(src, which, gain, shift, xhat, out, r), unroll=dims["unroll"])
+
+    need("tok")
+    for f in range(frames):
+        k.x32[f * ROWS : f * ROWS + patches, :] = k.tok[:, f, :].astype(FLOAT)
         set_tail(k.x32, f, [])
-    norm(k.x32, 0, t_gain, t_beta, k.xh_t, k.n_t)
-    l_ti.wait()
-
-    def to_slots(f, value, dst):
-        columns = value.shape[-1]
+    t_gain = vec("t_gain")
+    norm(k.x32, 0, t_gain, vec("t_beta"), k.xh_t, k.n_t)
+    need("w_ti")
+    t_qb = qkv_row("t_qv")
+
+    def frame(f):
+        return slice(f * ROWS, (f + 1) * ROWS)
+
+    def scatter(f, value, src, dst):
         moved = dot_nn(k.sel[...], value).astype(BHALF)
-        dst[:, :, f] = moved.reshape(seq, 2, HALF, columns)
-
-    def from_slots(f, src):
-        columns = src.shape[-1]
-        return dot_nn(k.les[...], src[:, :, f].reshape(seq * SLOTS, columns))
-
-    for f in range(frames):
-        r = slice(f * ROWS, (f + 1) * ROWS)
-        qkv = (dot_nn(k.n_t[r, :], k.w_ti[...]) + t_qb).astype(BHALF)
-        to_slots(f, qkv, k.q_send)
-    l_to.wait()
-    l_so.wait()
-    pl.semaphore_wait(barrier, len(everyone))
-    mine = pl.ds(frames * s, frames)
-
-    def scatter(src, dst):
-        copies = [send(src.at[p], dst.at[:, mine], (p, h)) for p in peers]
-        dst[:, mine] = src[s]
+        src[f] = moved.reshape(seq, 2, HALF, value.shape[-1])
+        to = frames * s + f
+        copies = [send(src.at[f, p], dst.at[:, to], (p, h)) for p in peers]
+        dst[:, to] = src[f, s]
         return copies
 
-    def gather(src, dst):
-        copies = [send(src.at[:, pl.ds(frames * p, frames)], dst.at[s], (p, h)) for p in peers]
-        dst[s] = src[:, mine]
+    def gather(b, src, dst):
+        copies = [send(src.at[b, pl.ds(frames * p, frames)], dst.at[b, s], (p, h)) for p in peers]
+        dst[b, s] = src[b, pl.ds(frames * s, frames)]
         return copies
+
+    def gathered(f, src):
+        return dot_nn(k.les[...], src[:, :, f].reshape(seq * SLOTS, src.shape[-1])).astype(BHALF)
 
     def arrived(copies):
         for copy in copies:
             copy.wait_recv()
 
-    q_copies = scatter(k.q_send, k.q_pos)
+    q_copies = []
+    for f in range(frames):
+        qkv = (dot_nt(k.n_t[frame(f), :], k.w_ti[...]) + t_qb).astype(BHALF)
+        if f == 0:
+            pl.semaphore_wait(barrier, len(everyone))
+        q_copies += scatter(f, qkv, k.q_send, k.q_pos)
 
     def share(ref):
         return send(ref.at[0, c], ref.at[0, c], sister), send(ref.at[0, c], ref.at[1, c], across)
@@ -759,13 +766,20 @@
     def pass_on(ref):
         return send(ref.at[1, c], ref.at[1, c], sister)
 
+    need("w_to", "w_so")
     w_to_near, w_to_far = share(k.w_to)
     w_so_near, w_so_far = share(k.w_so)
 
-    l_og.wait()
+    k.les[...] = chosen(iota((ROWS, seq * SLOTS), 1), iota((ROWS, seq * SLOTS), 0), False)
+    span = every * HALF
+    left, right = iota((span, span), 0), iota((span, span), 1)
+    same = (left % HALF == right % HALF) & (clip_of(left // HALF) == clip_of(right // HALF))
+    near = jnp.abs(left // HALF - right // HALF) < MAXLEN
+    k.tmask[...] = jnp.where(same & near, 0.0, NEG)
+    need("out_grad")
     cls_g = k.cls_grad[...].astype(FLOAT)
     for f in range(frames):
-        k.gr32[f * ROWS : f * ROWS + patches, :] = k.out_grad[f].astype(FLOAT)
+        k.gr32[f * ROWS : f * ROWS + patches, :] = k.out_grad[:, f, :].astype(FLOAT)
         set_tail(k.gr32, f, [cls_g] if f == 0 else [])
 
     def cast_rows(src, dst):
@@ -775,7 +789,7 @@
         blocks(body)
 
     cast_rows(k.gr32, k.gr16)
-    l_dn.wait()
+    need("w_dn")
     k.dact[...] = dot_nt(k.gr16[...], k.w_dn[...])
     w_to_far.wait_recv()
     w_to_last = pass_on(k.w_to)
@@ -802,18 +816,28 @@
         at = part * width + j * HEAD_DIM
         return value[:, at : at + HEAD_DIM]
 
-    arrived(q_copies)
-    for b in range(2):
-        qkv = k.q_pos[b].reshape(span, 3 * width)
+    def attend_all(qkv, mask, p_ref, first):
         out = [
-            attend(head_of(qkv, 0, j), head_of(qkv, 1, j), head_of(qkv, 2, j), k.tmask[...], k.p_t.at[b * heads + j])
+            attend(*[head_of(qkv, i, j) for i in range(3)], mask, p_ref.at[first + j]) for j in range(heads)
+        ]
+        return jnp.concatenate(out, axis=-1)
+
+    def attend_back_all(qkv, grad, p_ref, first):
+        out = [
+            attend_back(*[head_of(qkv, i, j) for i in range(3)], head_of(grad, 0, j), p_ref.at[first + j])
             for j in range(heads)
         ]
-        k.a_pos[b] = jnp.concatenate(out, axis=-1).reshape(every, HALF, width)
-    a_copies = gather(k.a_pos, k.a_recv)
+        return jnp.concatenate([out[j][i] for i in range(3) for j in range(heads)], axis=-1)
+
+    arrived(q_copies)
+    a_copies = []
+    for b in range(2):
+        out = attend_all(k.q_pos[b].reshape(span, 3 * width), k.tmask[...], k.p_t, b * heads)
+        k.a_pos[b] = out.reshape(every, HALF, width)
+        a_copies += gather(b, k.a_pos, k.a_recv)
     arrived(a_copies)
     for f in range(frames):
-        k.att_t[0, c, f * ROWS : (f + 1) * ROWS, :] = from_slots(f, k.a_recv).astype(BHALF)
+        k.att_t[0, c, frame(f), :] = gathered(f, k.a_recv)
 
     def project(att, weight):
         near, far = share(att)
@@ -826,12 +850,13 @@
 
     arrived([w_to_near, w_to_last])
     project(k.att_t, k.w_to)
+    t_ob, t_lb = vec("t_ob"), vec("t_lb")
 
     def mid_rows(r):
         k.mid16[r, :] = (k.t32[r, :] + k.u32[r, :] + t_ob).astype(BHALF)
 
     blocks(mid_rows)
-    l_tl.wait()
+    need("w_tl")
     k.t32[...] = dot_nn(k.mid16[...], k.w_tl[...])
 
     def add_res(r):
@@ -841,22 +866,18 @@
     for f in range(frames):
         set_tail(k.x32, f, [cls_row[f]])
 
-    norm(k.x32, 1, s_gain, s_beta, k.xh_s, k.n_s)
-    l_si.wait()
-    k.sqkv[...] = (dot_nn(k.n_s[...], k.w_si[...]) + s_qb).astype(BHALF)
+    s_gain = vec("s_gain")
+    norm(k.x32, 1, s_gain, vec("s_beta"), k.xh_s, k.n_s)
+    need("w_si")
+    k.sqkv[...] = (dot_nt(k.n_s[...], k.w_si[...]) + qkv_row("s_qv")).astype(BHALF)
     in_frame = jnp.where(iota((1, ROWS), 1) < patches + 1, 0.0, NEG)
     for f in range(frames):
-        r = slice(f * ROWS, (f + 1) * ROWS)
-        qkv = k.sqkv[r, :]
-        out = [
-            attend(head_of(qkv, 0, j), head_of(qkv, 1, j), head_of(qkv, 2, j), in_frame, k.p_s.at[f * heads + j])
-            for j in range(heads)
-        ]
-        k.att_s[0, c, r, :] = jnp.concatenate(out, axis=-1)
+        k.att_s[0, c, frame(f), :] = attend_all(k.sqkv[frame(f), :], in_frame, k.p_s, f * heads)
     arrived([w_so_near, w_so_last])
     project(k.att_s, k.w_so)
-    at = [slice(f * ROWS + patches, f * ROWS + patches + 1) for f in range(frames)]
-    space_cls = [k.t32[r, :] + k.u32[r, :] + s_ob for r in at]
+    s_ob = vec("s_ob")
+    cls_at = [slice(f * ROWS + patches, f * ROWS + patches + 1) for f in range(frames)]
+    space_cls = [k.t32[r, :] + k.u32[r, :] + s_ob for r in cls_at]
     parts = [sum(onehot[f][i] * space_cls[f] for f in range(frames)) for i in range(clips)]
     k.cls_send[...] = eight(parts)
     cls_copies = [send(k.cls_send, k.cls_recv.at[s], (p, h)) for p in peers]
@@ -866,18 +887,23 @@
         k.x32[r, :] = k.x32[r, :] + (k.t32[r, :] + k.u32[r, :] + s_ob)
 
     blocks(add_space)
+    for f in range(frames):
+        set_tail(k.x32, f, [])
+
+    m_gain, m_beta = vec("m_gain"), vec("m_beta")
+    norm(k.x32, 2, m_gain, m_beta, k.xh_m, k.n_m)
+    need("w_up")
+    k.t32[...] = dot_nn(k.n_m[...], k.w_up[...])
     arrived(cls_copies)
     cls_sum = k.cls_recv[0]
     for i in range(1, seq):
         cls_sum = cls_sum + k.cls_recv[i]
-    cls_mid = [cls32[i : i + 1] + cls_sum[i : i + 1] * per_len[i] for i in range(clips)]
-    for f in range(frames):
-        set_tail(k.x32, f, cls_mid if f == 0 else [])
-
-    norm(k.x32, 2, m_gain, m_beta, k.xh_m, k.n_m)
-    l_up.wait()
-    k.t32[...] = dot_nn(k.n_m[...], k.w_up[...])
+    set_tail(k.x32, 0, [cls32[i : i + 1] + cls_sum[i : i + 1] * per_len[i] for i in range(clips)])
+    last_block = slice(ROWS - HALF, ROWS)
+    norm_rows(k.x32, 2, m_gain, m_beta, k.xh_m, k.n_m, last_block)
+    k.t32[last_block, :] = dot_nn(k.n_m[last_block, :], k.w_up[...])
     first_seq = jnp.where(s == 0, 1.0, 0.0)
+    m_ub = vec("m_ub")
 
     def kept(r):
         at = r.start + iota((BLOCK, 1), 0)
@@ -897,10 +923,12 @@
 
     blocks(gelu_rows)
 
-    def sum_open(i, lhs, rhs, dot):
+    def sum_make(i, lhs, rhs, dot):
         for b in range(2):
             cut = slice(b * half, (b + 1) * half)
             k.part[i, b] = dot(lhs[...], rhs[cut, :] if dot is dot_nt else rhs[:, cut]).astype(BHALF)
+
+    def sum_open(i):
         return send(k.part.at[i, other_c], k.pair.at[i], sister)
 
     def sum_across(i, copy):
@@ -913,21 +941,28 @@
         k.total[i, c] = (k.part[i, c].astype(FLOAT) + k.other[i].astype(FLOAT)).astype(BHALF)
         return send(k.total.at[i, c], k.total.at[i, c], sister)
 
-    def sum_rows(i, r):
-        return jnp.concatenate([k.total[i, 0, r, :], k.total[i, 1, r, :]], axis=-1).astype(FLOAT)
-
-    def grad_open(name, lhs, rhs):
+    def rows_of(ref, r):
+        return jnp.concatenate([ref[0, r, :], ref[1, r, :]], axis=-1).astype(FLOAT)
+
+    def grad_make(name, lhs, rhs):
+        g = getattr(k, "g_" + name)
+        g[...] = dot_tn(lhs, rhs).astype(BHALF).reshape(g.shape)
+
+    def grad_open(name):
         g, got = getattr(k, "g_" + name), getattr(k, "y_" + name)
-        g[...] = dot_tn(lhs, rhs).astype(BHALF).reshape(g.shape)
-        return name, send(g.at[:, 1 - y], got, y_peer)
+        return name, [send(g.at[p, 1 - y], got.at[p], y_peer) for p in z_peers + [z]]
 
     def grad_along(job):
-        name, copy = job
+        name, opened = job
         g, got, last = [getattr(k, kind + name) for kind in ("g_", "y_", "z_")]
-        copy.wait_recv()
-        g[:, y] = (g[:, y].astype(FLOAT) + got[...].astype(FLOAT)).astype(BHALF)
-        last[z] = g[z, y]
-        return name, [send(g.at[p, y], last.at[z], (p * 2 + y, h)) for p in z_peers]
+        copies = []
+        for p, copy in zip(z_peers, opened):
+            copy.wait_recv()
+            g[p, y] = (g[p, y].astype(FLOAT) + got[p].astype(FLOAT)).astype(BHALF)
+            copies.append(send(g.at[p, y], last.at[z], (p * 2 + y, h)))
+        opened[-1].wait_recv()
+        last[z] = (g[z, y].astype(FLOAT) + got[z].astype(FLOAT)).astype(BHALF)
+        return name, copies
 
     def grad_close(job):
         name, copies = job
@@ -958,40 +993,41 @@
             out = jnp.concatenate([out, jnp.zeros((1, model - out.shape[1]), FLOAT)], axis=-1)
         return out
 
+    def block_sums(body):
+        def step(b, sums):
+            pair = body(pl.ds(pl.multiple_of(b * BLOCK, BLOCK), BLOCK))
+            return tuple(t + jnp.sum(v.reshape(BLOCK // 8, 8, model), axis=0) for t, v in zip(sums, pair))
+
+        zero = jnp.zeros((8, model), FLOAT)
+        sums = lax.fori_loop(0, rows // BLOCK, step, (zero, zero))
+        return [jnp.sum(v, axis=0, keepdims=True) for v in sums]
+
     def norm_back(i, which, gain, xhat, keep, use):
-        def body(r, sums):
-            g = sum_rows(i, r)
+        def body(r):
+            g = rows_of(k.total.at[i], r)
             n = xhat[r, :]
             gh = g * gain
             m1 = jnp.mean(gh, axis=-1, keepdims=True)
             m2 = jnp.mean(gh * n, axis=-1, keepdims=True)
             use(r, k.inv[which, r, 0:1] * (gh - m1 - n * m2))
             w = g * kept(r) if keep else g
-            fold = lambda v: jnp.sum(v.reshape(BLOCK // 8, 8, model), axis=0)
-            return sums[0] + fold(w * n), sums[1] + fold(w)
-
-        zero = jnp.zeros((8, model), FLOAT)
-        sums = (zero, zero)
-        if dims["unroll"]:
-            for b in range(rows // BLOCK):
-                sums = body(pl.ds(b * BLOCK, BLOCK), sums)
-        else:
-            sums = lax.fori_loop(
-                0, rows // BLOCK, lambda b, v: body(pl.ds(pl.multiple_of(b * BLOCK, BLOCK), BLOCK), v), sums
-            )
-        return [jnp.sum(v, axis=0, keepdims=True) for v in sums]
-
-    m_sum = sum_open(0, k.gpre, k.w_up, dot_nt)
-    j_dn = grad_open("dn", k.gr16[...], k.act_k[...])
+            return w * n, w
+
+        return block_sums(body)
+
+    sum_make(0, k.gpre, k.w_up, dot_nt)
+    m_sum = sum_open(0)
+    grad_make("dn", k.gr16[...], k.act_k[...])
     m_sum = sum_across(0, m_sum)
-    j_up = grad_open("up", k.n_m[...], k.gpre_k[...])
-    o_sum = sum_open(1, k.act, k.w_dn, dot_nn)
-    j_dn = grad_along(j_dn)
+    j_dn = grad_open("dn")
+    grad_make("up", k.n_m[...], k.gpre_k[...])
+    j_up = grad_open("up")
+    sum_make(1, k.act, k.w_dn, dot_nn)
+    o_sum = sum_open(1)
+    ub_grad, db_grad = col_sums(k.gpre_k), col_sums(k.gr16, ones_kept)
+    m_last = sum_close(0, m_sum)
     o_sum = sum_across(1, o_sum)
-    ub_grad, db_grad = col_sums(k.gpre_k), col_sums(k.gr16, ones_kept)
-    j_up = grad_along(j_up)
-    last = sum_close(0, m_sum)
-    last.wait_recv()
+    m_last.wait_recv()
 
     def use_m(r, dx):
         k.gr32[r, :] = k.gr32[r, :] + dx
@@ -1009,117 +1045,133 @@
 
     k.gatt[...] = dot_nt(k.gss[...], k.w_so[0, c]).astype(BHALF)
     for f in range(frames):
-        r = slice(f * ROWS, (f + 1) * ROWS)
-        qkv, grad = k.sqkv[r, :], k.gatt[r, :]
-        out = [
-            attend_back(*[head_of(qkv, i, j) for i in range(3)], head_of(grad, 0, j), k.p_s.at[f * heads + j])
-            for j in range(heads)
-        ]
-        k.dsq[r, :] = jnp.concatenate([out[j][i] for i in range(3) for j in range(heads)], axis=-1)
-    s_sum = sum_open(2, k.dsq, k.w_si, dot_nt)
-    j_si = grad_open("si", k.n_s[...], k.dsq[...])
+        k.dsq[frame(f), :] = attend_back_all(k.sqkv[frame(f), :], k.gatt[frame(f), :], k.p_s, f * heads)
+    sum_make(2, k.dsq, k.w_si, dot_nn)
+    s_sum = sum_open(2)
+    j_dn = grad_along(j_dn)
     s_sum = sum_across(2, s_sum)
-    last = sum_close(1, o_sum)
-    j_so = grad_open("so", k.gss[...], k.att_s[0, c])
-    j_si = grad_along(j_si)
-    last.wait_recv()
+    grad_make("si", k.n_s[...], k.dsq[...])
+    j_si = grad_open("si")
+    grad_make("so", k.gss[...], k.att_s[0, c])
+    j_so = grad_open("so")
+    o_last = sum_close(1, o_sum)
+    s_rows = [col_sums(k.gss), col_sums(k.dsq)]
+    j_up = grad_along(j_up)
+    o_last.wait_recv()
+    m_db = vec("m_db")
 
     def out_rows(r):
-        k.t32[r, :] = k.x32[r, :] + sum_rows(1, r) + m_db
+        k.t32[r, :] = k.x32[r, :] + rows_of(k.total.at[1], r) + m_db
 
     blocks(out_rows)
     for f in range(frames):
-        k.o_blk[f] = k.t32[f * ROWS : f * ROWS + patches, :].astype(BHALF)
+        k.o_blk[:, f, :] = k.t32[f * ROWS : f * ROWS + patches, :].astype(BHALF)
     k.o_cls[...] = k.t32[patches : patches + clips, :].astype(BHALF)
-    s_rows = [col_sums(k.gss), col_sums(k.dsq)]
-    j_so = grad_along(j_so)
-    last = sum_close(2, s_sum)
-    last.wait_recv()
+    s_last = sum_close(2, s_sum)
+    s_last.wait_recv()
     sums = norm_back(2, 1, s_gain, k.xh_s, False, use_m)
-    cls_in = [k.gr32[f * ROWS + patches : f * ROWS + patches + 1, :] for f in range(frames)]
+    cls_in = [k.gr32[r, :] for r in cls_at]
     cls_parts = [sum(onehot[f][i] * cls_in[f] for f in range(frames)) for i in range(clips)]
     for f in range(frames):
         set_tail(k.gr32, f, [])
-    v_s = vectors_send(1, [sums[0], sums[1]] + s_rows + cls_parts)
     cast_rows(k.gr32, k.gtr)
 
     k.gtm[...] = dot_nt(k.gtr[...], k.w_tl[...]).astype(BHALF)
     k.gatt[...] = dot_nt(k.gtm[...], k.w_to[0, c]).astype(BHALF)
-    for f in range(frames):
-        to_slots(f, k.gatt[f * ROWS : (f + 1) * ROWS, :], k.g_send)
-    g_copies = scatter(k.g_send, k.g_pos)
+    g_copies = []
+    for f in range(frames):
+        g_copies += scatter(f, k.gatt[frame(f), :], k.g_send, k.g_pos)
+    v_s = vectors_send(1, [sums[0], sums[1]] + s_rows + cls_parts)
     pick = (iota((model, width), 0) == h * width + iota((model, width), 1)).astype(FLOAT).astype(BHALF)
-    j_tl = grad_open("tl", k.mid16[...], dot_nn(k.gtr[...], pick).astype(BHALF))
-    j_to = grad_open("to", k.gtm[...], k.att_t[0, c])
+    grad_make("tl", k.mid16[...], dot_nn(k.gtr[...], pick).astype(BHALF))
+    grad_make("to", k.gtm[...], k.att_t[0, c])
     t_rows = [col_sums(k.gtm), col_sums(k.gtr)]
     arrived(g_copies)
+    d_copies = []
     for b in range(2):
-        qkv, grad = k.q_pos[b].reshape(span, 3 * width), k.g_pos[b].reshape(span, width)
-        out = [
-            attend_back(*[head_of(qkv, i, j) for i in range(3)], head_of(grad, 0, j), k.p_t.at[b * heads + j])
-            for j in range(heads)
-        ]
-        value = jnp.concatenate([out[j][i] for i in range(3) for j in range(heads)], axis=-1)
+        value = attend_back_all(
+            k.q_pos[b].reshape(span, 3 * width), k.g_pos[b].reshape(span, width), k.p_t, b * heads
+        )
         k.d_pos[b] = value.reshape(every, HALF, 3 * width)
-    d_copies = gather(k.d_pos, k.d_recv)
+        d_copies += gather(b, k.d_pos, k.d_recv)
+    j_tl = grad_open("tl")
+    j_to = grad_open("to")
+    j_si = grad_along(j_si)
+    j_so = grad_along(j_so)
+    grad_close(j_dn)
+    m_vec = vectors_close(0, v_m)
+    s_vec = vectors_close(1, v_s)
+    k.o_vec[0:8, :] = m_vec
+    k.o_vec[8:16, :] = s_vec + jnp.concatenate([jnp.zeros((4, model), FLOAT), k.gcm[0:4, :]], axis=0)
+    arrived(d_copies)
+    for f in range(frames):
+        k.dtq[frame(f), :] = gathered(f, k.d_recv)
+    sum_make(3, k.dtq, k.w_ti, dot_nn)
+    t_sum = sum_open(3)
+    grad_make("ti", k.n_t[...], k.dtq[...])
+    j_ti = grad_open("ti")
+
+    def partial(r):
+        g = rows_of(k.part.at[3], r)
+        return g * k.xh_t[r, :], g
+
+    sums = block_sums(partial)
+    t_sum = sum_across(3, t_sum)
+    v_t = vectors_send(2, [sums[0], sums[1], t_rows[0], col_sums(k.dtq), t_rows[1]])
     j_tl = grad_along(j_tl)
     j_to = grad_along(j_to)
-    grad_close(j_dn)
     grad_close(j_up)
-    m_vec = vectors_close(0, v_m)
-    s_vec = vectors_close(1, v_s)
-    arrived(d_copies)
-    for f in range(frames):
-        k.dtq[f * ROWS : (f + 1) * ROWS, :] = from_slots(f, k.d_recv).astype(BHALF)
-    t_sum = sum_open(3, k.dtq, k.w_ti, dot_nt)
-    j_ti = grad_open("ti", k.n_t[...], k.dtq[...])
-    t_sum = sum_across(3, t_sum)
-    pair_row = col_sums(k.dtq)
     grad_close(j_si)
     grad_close(j_so)
+    t_vec = vectors_close(2, v_t)
+    k.v_head[h] = t_vec
+    h_copies = [send(k.v_head.at[h], k.v_head.at[h], device) for device in (sister, across, diagonal)]
     j_ti = grad_along(j_ti)
+    t_last = sum_close(3, t_sum)
     grad_close(j_tl)
     grad_close(j_to)
-    last = sum_close(3, t_sum)
-    last.wait_recv()
+    t_last.wait_recv()
 
     def use_t(r, dx):
         k.t32[r, :] = k.gr32[r, :] + dx.astype(BHALF).astype(FLOAT)
 
-    sums = norm_back(3, 0, t_gain, k.xh_t, False, use_t)
-    v_t = vectors_send(2, [sums[0], sums[1], t_rows[0], pair_row, t_rows[1]])
-    for f in range(frames):
-        k.o_tok[f] = k.t32[f * ROWS : f * ROWS + patches, :].astype(BHALF)
-    k.o_vec[0:8, :] = m_vec
-    k.o_vec[8:16, :] = s_vec + jnp.concatenate([jnp.zeros((4, model), FLOAT), k.gcm[0:4, :]], axis=0)
-    k.o_vec[16:24, :] = vectors_close(2, v_t)
+    norm_back(3, 0, t_gain, k.xh_t, False, use_t)
+    for f in range(frames):
+        k.o_tok[:, f, :] = k.t32[f * ROWS : f * ROWS + patches, :].astype(BHALF)
+    arrived(h_copies)
+    over_head = k.v_head[0] + k.v_head[1] + k.v_head[2] + k.v_head[3]
+    k.o_vec[16:24, :] = jnp.concatenate([over_head[0:2], t_vec[2:8]], axis=0)
     grad_close(j_ti)
     for copy in unsent:
         copy.wait_send()
 
 
-def finish_kernel(dims, vec, g_dn, g_up, g_si, g_so, g_tl, g_to, g_ti, *outs):
+def finish_kernel(dims, h_blk, h_tok, vec, cls_out, g_dn, g_up, g_si, g_so, g_tl, g_to, g_ti, *refs):
     width, model, seq = dims["width"], dims["model"], dims["seq"]
     share, clips = model // seq, dims["clips"]
-    cls, tg, tb, ti, tp, to, tob, tl, tlb, sg, sb, si, sp, so, sob, mg, mb, up, ub, dn, db = outs
+    o_blk, o_cls, o_tok, cls, tg, tb, ti, tp, to, tob, tl, tlb, sg, sb, si, sp, so, sob, mg, mb, up, ub, dn, db = refs
+    o_blk[...] = h_blk[...]
+    o_tok[...] = h_tok[...]
     s = lax.axis_index("seq")
     v = vec[...]
     mine = pltpu.roll(v, (model - share * s) % model, 1)[:, :share]
-    mg[...], mb[...], ub[...], db[...] = mine[0:1], v[1:2], v[2:3], v[3:4]
-    sg[...], sb[...], sob[...] = mine[8:9], v[9:10], v[10:11]
-    tg[...], tb[...], tob[...], tlb[...] = mine[16:17], v[17:18], v[18:19], v[20:21]
+    for out, row in ((mg, 0), (sg, 8), (tg, 16)):
+        out[...] = mine[row : row + 1].reshape(share)
+    for out, row in ((mb, 1), (ub, 2), (db, 3), (sb, 9), (sob, 10), (tb, 17), (tob, 18), (tlb, 20)):
+        out[...] = v[row : row + 1].reshape(model)
     cls[...] = mine[12 : 12 + clips]
+    o_cls[...] = cls_out[...]
     for out, row in ((sp, 11), (tp, 19)):
         out[0:1, :] = v[row : row + 1, :width]
         out[1:2, :] = v[row : row + 1, 2 * width : 3 * width]
     for out, g in ((si, g_si), (ti, g_ti)):
         for i in range(3):
-            out[:, i, :] = g[:, i * width : (i + 1) * width]
+            out[i] = g[:, i * width : (i + 1) * width]
     tl[...] = g_tl[...]
     up[...] = g_up[...]
+    dn[...] = g_dn[...]
     to[...] = g_to[...].T
     so[...] = g_so[...].T
-    dn[...] = g_dn[...].T
 
 
 def fused_body(
@@ -1164,42 +1216,29 @@
         unroll=False,
     )
 
-    def wide(v):
-        return jnp.pad(v, (0, model - v.shape[0]))
-
-    vec = jnp.stack(
-        [
-            time_gain,
-            time_beta,
-            time_out_bias,
-            time_linear_bias,
-            space_gain,
-            space_beta,
-            space_out_bias,
-            mlp_gain,
-            mlp_beta,
-            mlp_down_bias,
-            mlp_up_bias,
-            wide(qkv_shift(time_qv_bias)),
-            wide(qkv_shift(space_qv_bias)),
-        ]
-    )
+    def frames_inner(v):
+        return jnp.transpose(v, (1, 0, 2))
+
+    def outputs_first(v):
+        return jnp.transpose(v, (1, 2, 0)).reshape(3 * width, model)
+
     scratch = scratch_shapes(dims)
     grads = grad_columns(dims)
     share = model // seq
     shape = jax.ShapeDtypeStruct
     vmem, anywhere = pl.BlockSpec(memory_space=pltpu.VMEM), pl.BlockSpec(memory_space=pl.ANY)
+    inner = (patches, frames, model)
     outs = [
-        shape(tokens.shape, BHALF),
+        shape(inner, BHALF),
         shape(cls_tokens.shape, BHALF),
-        shape(tokens.shape, BHALF),
+        shape(inner, BHALF),
         shape((24, model), FLOAT),
     ] + [shape((share, columns), FLOAT) for _, columns in grads]
     names = list(INPUTS) + list(OUTPUTS) + ["o_" + name for name, _ in grads] + list(scratch)
     results = pl.pallas_call(
         functools.partial(layer_kernel, dims, names),
         out_shape=outs,
-        in_specs=[pl.BlockSpec(memory_space=pltpu.SMEM)] + [vmem] * 3 + [anywhere] * 9,
+        in_specs=[pl.BlockSpec(memory_space=pltpu.SMEM)] + [vmem] * 2 + [anywhere] * (len(INPUTS) - 3),
         out_specs=[vmem] * len(outs),
         scratch_shapes=list(scratch.values()),
         compiler_params=pltpu.CompilerParams(
@@ -1210,21 +1249,36 @@
         clip_lengths,
         cls_tokens,
         cls_grad,
-        vec,
-        tokens,
-        out_grad,
-        time_proj_in.reshape(model, 3 * width),
+        time_gain,
+        time_beta,
+        time_out_bias,
+        time_linear_bias,
+        space_gain,
+        space_beta,
+        space_out_bias,
+        mlp_gain,
+        mlp_beta,
+        mlp_down_bias,
+        mlp_up_bias,
+        time_qv_bias,
+        space_qv_bias,
+        frames_inner(tokens),
+        frames_inner(out_grad),
+        outputs_first(time_proj_in),
         time_proj_out,
         time_linear,
-        space_proj_in.reshape(model, 3 * width),
+        outputs_first(space_proj_in),
         space_proj_out,
         mlp_up,
         mlp_down,
     )
-    block_out, cls_out, tokens_grad = results[:3]
-    row, gain = shape((1, model), FLOAT), shape((1, share), FLOAT)
-    proj, pair = shape((share, 3, width), FLOAT), shape((2, width), FLOAT)
+    blk, cls_out, tok, vectors = results[:4]
+    row, gain = shape((model,), FLOAT), shape((share,), FLOAT)
+    proj, pair = shape((3, share, width), FLOAT), shape((2, width), FLOAT)
     out_shape = [
+        shape(inner, BHALF),
+        shape(cls_tokens.shape, BHALF),
+        shape(inner, BHALF),
         shape((clips, share), FLOAT),
         gain,
         row,
@@ -1243,20 +1297,23 @@
         gain,
         row,
         shape((share, hidden), FLOAT),
-        shape((1, hidden), FLOAT),
-        shape((hidden, share), FLOAT),
+        shape((hidden,), FLOAT),
+        shape((share, hidden), FLOAT),
         row,
     ]
     last = pl.pallas_call(
         functools.partial(finish_kernel, dims),
         out_shape=out_shape,
-        in_specs=[vmem] * 8,
+        in_specs=[vmem] * 11,
         out_specs=[vmem] * len(out_shape),
-        compiler_params=pltpu.CompilerParams(vmem_limit_bytes=32 * 1024 * 1024),
+        compiler_params=pltpu.CompilerParams(vmem_limit_bytes=62 * 1024 * 1024),
         name="finish",
-    )(*results[3:])
-    last = [v.reshape(-1) if v.shape[0] == 1 else v for v in last]
-    return (block_out, cls_out, tokens_grad, *last)
+    )(blk, tok, vectors, cls_out, *results[4:])
+    last = list(last)
+    for i in (0, 2, 6, 14):
+        last[i] = jnp.transpose(last[i], (1, 0, 2))
+    last[22] = last[22].T
+    return tuple(last)
 
 
 def solution(mesh):

time: 224 us -> 180 us (0.80)
  local copies, waits for them, and re-layouts: 22.3 us -> 0 us
  Pallas kernels: 196 us -> 179 us
  other arithmetic: 4.91 us -> 0 us
    pallas_call x1, Pallas kernels: 195 us -> 176 us  [fused_body(): pl.pallas_call(functools.partial(layer_kernel, dims, names), out_shape=ou...]
    unnamed x34 -> x0, local copies, waits for them, and re-layouts: 9.75 us -> none
    another operation x15 -> x0, local copies, waits for them, and re-layouts: 9 us -> none  [the longest x14 8.92 us: fused_body(): jnp.stack([time_gain, time_beta, time_out_bias, time_linear_bias, space_g...]
    pallas_call x8 -> x0, other arithmetic: 4.84 us -> none  [fused_body(): pl.pallas_call(functools.partial(finish_kernel, dims), out_shape=out_shap...]
    reshape x4 -> x0, local copies, waits for them, and re-layouts: 2.8 us -> none  [the longest x1 1.32 us: fused_body(): time_proj_in.reshape(model, 3 * width)]
    pallas_call x1, Pallas kernels: 1.23 us -> 3.49 us  [fused_body(): pl.pallas_call(functools.partial(finish_kernel, dims), out_shape=out_shap...]
where the time goes in v2:
time: 180 us
  Pallas kernels  179 us (99%)
    pallas_call x1, Pallas kernels, fused_body(): pl.pallas_call(functools.partial(layer_kernel, dims, names), out_shape=ou...  176 us

profile of v2, /device:TPU:0, one launch (start us, length us, event | category | flops | bytes accessed | tf_op | source)
XLA Modules:
  0.0 180.0 jit_solution(12768783344359652913)
XLA Ops:
  0.7 175.7 %layer.1 = (bf16[196,2,768]{2,1,0:T(2,128)(2,1)}, bf16[4,768]{1,0:T(4,128)(2,1)}, bf16[196,2,768]{2,1,0:T(2,128)(2,1)}, f32[24,768]{1,0:T(8,128)}, f32[96,768]{1...) custom-call(s32[4]{0:T(128)} %refs_0_.1, ...), custom_call_target="tpu_custom_call" | custom-call | tf_op jit(solution)/shard_map/layer/pallas_call | solution.py:1238
  176.4 3.5 %finish.1 = (bf16[196,2,768]{2,1,0:T(2,128)(2,1)}, bf16[4,768]{1,0:T(4,128)(2,1)}, bf16[196,2,768]{2,1,0:T(2,128)(2,1)}, f32[4,96]{1,0:T(4,128)}, f32[96]{0:T(12...) custom-call(bf16[196,2,768]{2,1,0:T(2,128)(2,1)} %get-tuple-element., ...), custom_call_target="tpu_custom_call" | custom-call | tf_op jit(solution)/shard_map/finish/pallas_call | solution.py:1304

commit v3 on v2

--- a/solution.py
+++ b/solution.py
@@ -470,7 +470,6 @@
 ROWS = 208
 HALF = 16
 SLOTS = 2 * HALF
-BLOCK = 32
 
 
 def dot_nn(left, right):
@@ -556,16 +555,18 @@
         v_head=vm((4, 8, model), FLOAT),
     )
     for name, columns in grad_columns(dims):
-        shapes["g_" + name] = vm((seq // 2, 2, model // seq, columns), low)
-        shapes["y_" + name] = vm((seq // 2, model // seq, columns), low)
-        shapes["z_" + name] = vm((seq // 2, model // seq, columns), low)
+        share = model // seq
+        shapes["g_" + name] = vm((seq // 4, 2, 2, share, columns), low)
+        shapes["y_" + name] = vm((2, seq // 4, share, columns), low)
+        shapes["z_" + name] = vm((seq // 4, share, columns), low)
+        shapes["x_" + name] = vm((share, columns), low)
     for name in VECTORS:
         shapes[name] = vm((hidden if name == "m_ub" else model,), FLOAT)
     for name in PAIRS:
         shapes[name] = vm((2, width), FLOAT)
     shapes["load"] = pltpu.SemaphoreType.DMA((32,))
-    shapes["sent"] = pltpu.SemaphoreType.DMA((240,))
-    shapes["got"] = pltpu.SemaphoreType.DMA((240,))
+    shapes["sent"] = pltpu.SemaphoreType.DMA((280,))
+    shapes["got"] = pltpu.SemaphoreType.DMA((280,))
     return shapes
 
 
@@ -574,11 +575,10 @@
     return (
         ("dn", hidden),
         ("up", hidden),
-        ("si", 3 * width),
-        ("so", width),
-        ("tl", width),
-        ("to", width),
-        ("ti", 3 * width),
+        ("s", 4 * width),
+        ("l", 2 * width),
+        ("ta", 2 * width),
+        ("tb", width),
     )
 
 
@@ -591,6 +591,11 @@
 
 class Refs:
     pass
+
+
+class Exchange:
+    def __init__(self, out, into):
+        self.wait_send, self.wait_recv = out.wait_send, into.wait_recv
 
 
 def layer_kernel(dims, names, *refs):
@@ -601,6 +606,7 @@
     patches, clips, pos = dims["patches"], dims["clips"], dims["pos"]
     rows, every, heads, half = frames * ROWS, frames * seq, width // HEAD_DIM, model // 2
     zs = seq // 2
+    share_rows = model // seq
     scale = HEAD_DIM ** (-0.5)
     s, h = lax.axis_index("seq"), lax.axis_index("head")
     z, y = s // 2, s % 2
@@ -608,22 +614,17 @@
     other_c = 1 - c
     sister, across, diagonal = (s, x * 2 + other_c), (s, (1 - x) * 2 + c), (s, (1 - x) * 2 + other_c)
     y_peer = (z * 2 + 1 - y, h)
-    z_peers = [((z + i) % zs) for i in range(1, zs)]
     peers = [((z + i) % zs) * 2 + (y + j) % 2 for i in range(zs) for j in range(2) if i or j]
+    givers = [((z + zs - i) % zs) * 2 + (y + j) % 2 for i in range(zs) for j in range(2) if i or j]
     used = [0]
 
-    def send(src, dst, device):
+    def send(src, dst, device, lands):
         index = used[0]
         used[0] += 1
-        copy = pltpu.make_async_remote_copy(
-            src_ref=src,
-            dst_ref=dst,
-            send_sem=k.sent.at[index],
-            recv_sem=k.got.at[index],
-            device_id=device,
-            device_id_type=MESH,
-        )
+        sems = dict(send_sem=k.sent.at[index], recv_sem=k.got.at[index], device_id=device, device_id_type=MESH)
+        copy = pltpu.make_async_remote_copy(src_ref=src, dst_ref=dst, **sems)
         copy.start()
+        copy = Exchange(copy, pltpu.make_async_remote_copy(src_ref=src, dst_ref=lands, **sems))
         unsent.append(copy)
         return copy
 
@@ -635,18 +636,6 @@
         loads[0] += 1
         copy.start()
         return copy
-
-    def blocks(body, unroll=False):
-        if unroll:
-            for i in range(rows // BLOCK):
-                body(pl.ds(i * BLOCK, BLOCK))
-        else:
-
-            def step(i, carry):
-                body(pl.ds(pl.multiple_of(i * BLOCK, BLOCK), BLOCK))
-                return carry
-
-            lax.fori_loop(0, rows // BLOCK, step, 0)
 
     places = {"w_to": k.w_to.at[0, c], "w_so": k.w_so.at[0, c]}
     order = ("tok", "t_gain", "t_beta", "w_ti", "t_qv", "w_to", "w_so", "out_grad", "w_dn") + VECTORS[2:] + ("s_qv", "w_tl", "w_si", "w_up")
@@ -709,7 +698,10 @@
         fill = [jnp.zeros((missing, model), FLOAT)] if missing else []
         return jnp.concatenate(list(values) + fill, axis=0)
 
-    def norm_rows(src, which, gain, shift, xhat, out, r):
+    def frame(f):
+        return slice(f * ROWS, (f + 1) * ROWS)
+
+    def norm(src, which, gain, shift, xhat, out, r):
         v = src[r, :]
         center = v - jnp.mean(v, axis=-1, keepdims=True)
         invstd = lax.rsqrt(jnp.mean(center * center, axis=-1, keepdims=True) + EPS)
@@ -718,53 +710,53 @@
         k.inv[which, r, :] = jnp.broadcast_to(invstd, (v.shape[0], 128))
         out[r, :] = (n * gain + shift).astype(BHALF)
 
-    def norm(src, which, gain, shift, xhat, out):
-        blocks(lambda r: norm_rows(src, which, gain, shift, xhat, out, r), unroll=dims["unroll"])
-
-    need("tok")
-    for f in range(frames):
-        k.x32[f * ROWS : f * ROWS + patches, :] = k.tok[:, f, :].astype(FLOAT)
-        set_tail(k.x32, f, [])
-    t_gain = vec("t_gain")
-    norm(k.x32, 0, t_gain, vec("t_beta"), k.xh_t, k.n_t)
-    need("w_ti")
-    t_qb = qkv_row("t_qv")
-
-    def frame(f):
-        return slice(f * ROWS, (f + 1) * ROWS)
+    def arrived(copies):
+        for copy in copies:
+            copy.wait_recv()
 
     def scatter(f, value, src, dst):
         moved = dot_nn(k.sel[...], value).astype(BHALF)
         src[f] = moved.reshape(seq, 2, HALF, value.shape[-1])
         to = frames * s + f
-        copies = [send(src.at[f, p], dst.at[:, to], (p, h)) for p in peers]
+        copies = [
+            [send(src.at[f, p, b], dst.at[b, to], (p, h), dst.at[b, frames * q + f]) for p, q in zip(peers, givers)]
+            for b in range(2)
+        ]
         dst[:, to] = src[f, s]
         return copies
 
     def gather(b, src, dst):
-        copies = [send(src.at[b, pl.ds(frames * p, frames)], dst.at[b, s], (p, h)) for p in peers]
+        copies = [
+            send(src.at[b, pl.ds(frames * p, frames)], dst.at[b, s], (p, h), dst.at[b, q]) for p, q in zip(peers, givers)
+        ]
         dst[b, s] = src[b, pl.ds(frames * s, frames)]
         return copies
 
     def gathered(f, src):
         return dot_nn(k.les[...], src[:, :, f].reshape(seq * SLOTS, src.shape[-1])).astype(BHALF)
 
-    def arrived(copies):
-        for copy in copies:
-            copy.wait_recv()
-
+    need("tok")
+    t_gain, t_beta, t_qb = vec("t_gain"), vec("t_beta"), qkv_row("t_qv")
     q_copies = []
     for f in range(frames):
+        k.x32[f * ROWS : f * ROWS + patches, :] = k.tok[:, f, :].astype(FLOAT)
+        set_tail(k.x32, f, [])
+        norm(k.x32, 0, t_gain, t_beta, k.xh_t, k.n_t, frame(f))
+        if f == 0:
+            need("w_ti")
         qkv = (dot_nt(k.n_t[frame(f), :], k.w_ti[...]) + t_qb).astype(BHALF)
         if f == 0:
             pl.semaphore_wait(barrier, len(everyone))
-        q_copies += scatter(f, qkv, k.q_send, k.q_pos)
+        q_copies.append(scatter(f, qkv, k.q_send, k.q_pos))
 
     def share(ref):
-        return send(ref.at[0, c], ref.at[0, c], sister), send(ref.at[0, c], ref.at[1, c], across)
+        return (
+            send(ref.at[0, c], ref.at[0, c], sister, ref.at[0, other_c]),
+            send(ref.at[0, c], ref.at[1, c], across, ref.at[1, c]),
+        )
 
     def pass_on(ref):
-        return send(ref.at[1, c], ref.at[1, c], sister)
+        return send(ref.at[1, c], ref.at[1, c], sister, ref.at[1, other_c])
 
     need("w_to", "w_so")
     w_to_near, w_to_far = share(k.w_to)
@@ -781,14 +773,7 @@
     for f in range(frames):
         k.gr32[f * ROWS : f * ROWS + patches, :] = k.out_grad[:, f, :].astype(FLOAT)
         set_tail(k.gr32, f, [cls_g] if f == 0 else [])
-
-    def cast_rows(src, dst):
-        def body(r):
-            dst[r, :] = src[r, :].astype(BHALF)
-
-        blocks(body)
-
-    cast_rows(k.gr32, k.gr16)
+        k.gr16[frame(f), :] = k.gr32[frame(f), :].astype(BHALF)
     need("w_dn")
     k.dact[...] = dot_nt(k.gr16[...], k.w_dn[...])
     w_to_far.wait_recv()
@@ -829,84 +814,92 @@
         ]
         return jnp.concatenate([out[j][i] for i in range(3) for j in range(heads)], axis=-1)
 
-    arrived(q_copies)
     a_copies = []
     for b in range(2):
+        for copies in q_copies:
+            arrived(copies[b])
         out = attend_all(k.q_pos[b].reshape(span, 3 * width), k.tmask[...], k.p_t, b * heads)
         k.a_pos[b] = out.reshape(every, HALF, width)
         a_copies += gather(b, k.a_pos, k.a_recv)
     arrived(a_copies)
+
+    def features(f, att):
+        r = frame(f)
+        return (
+            send(att.at[0, c, r], att.at[0, c, r], sister, att.at[0, other_c, r]),
+            send(att.at[0, c, r], att.at[1, c, r], across, att.at[1, c, r]),
+        )
+
+    def own_part(f, att, weight, copies):
+        r = frame(f)
+        copies[0].wait_recv()
+        k.t32[r, :] = dot_nn(att[0, 0, r], weight[0, 0]) + dot_nn(att[0, 1, r], weight[0, 1])
+
+    def features_on(f, att, copies):
+        copies[1].wait_recv()
+        r = frame(f)
+        return send(att.at[1, c, r], att.at[1, c, r], sister, att.at[1, other_c, r])
+
+    def both_parts(f, att, weight, copy):
+        r = frame(f)
+        copy.wait_recv()
+        k.u32[r, :] = dot_nn(att[1, 0, r], weight[1, 0]) + dot_nn(att[1, 1, r], weight[1, 1])
+        own, other = k.t32[r, :], k.u32[r, :]
+        return jnp.where(x == 0, own, other) + jnp.where(x == 0, other, own)
+
+    ta_copies = []
     for f in range(frames):
         k.att_t[0, c, frame(f), :] = gathered(f, k.a_recv)
-
-    def project(att, weight):
-        near, far = share(att)
-        near.wait_recv()
-        k.t32[...] = dot_nn(att[0, 0], weight[0, 0]) + dot_nn(att[0, 1], weight[0, 1])
-        far.wait_recv()
-        last = pass_on(att)
-        last.wait_recv()
-        k.u32[...] = dot_nn(att[1, 0], weight[1, 0]) + dot_nn(att[1, 1], weight[1, 1])
-
+        ta_copies.append(features(f, k.att_t))
     arrived([w_to_near, w_to_last])
-    project(k.att_t, k.w_to)
-    t_ob, t_lb = vec("t_ob"), vec("t_lb")
-
-    def mid_rows(r):
-        k.mid16[r, :] = (k.t32[r, :] + k.u32[r, :] + t_ob).astype(BHALF)
-
-    blocks(mid_rows)
-    need("w_tl")
-    k.t32[...] = dot_nn(k.mid16[...], k.w_tl[...])
-
-    def add_res(r):
-        k.x32[r, :] = k.x32[r, :] + (k.t32[r, :] + t_lb).astype(BHALF).astype(FLOAT)
-
-    blocks(add_res)
-    for f in range(frames):
+    t_ob, t_lb, s_gain, s_beta, s_qb = vec("t_ob"), vec("t_lb"), vec("s_gain"), vec("s_beta"), qkv_row("s_qv")
+    need("w_tl", "w_si")
+    in_frame = jnp.where(iota((1, ROWS), 1) < patches + 1, 0.0, NEG)
+    for f in range(frames):
+        own_part(f, k.att_t, k.w_to, ta_copies[f])
+    ta_last, sa_copies = [], []
+    for f in range(frames):
+        ta_last.append(features_on(f, k.att_t, ta_copies[f]))
+    for f in range(frames):
+        r = frame(f)
+        k.mid16[r, :] = (both_parts(f, k.att_t, k.w_to, ta_last[f]) + t_ob).astype(BHALF)
+        res = (dot_nn(k.mid16[r, :], k.w_tl[...]) + t_lb).astype(BHALF)
+        k.x32[r, :] = k.x32[r, :] + res.astype(FLOAT)
         set_tail(k.x32, f, [cls_row[f]])
-
-    s_gain = vec("s_gain")
-    norm(k.x32, 1, s_gain, vec("s_beta"), k.xh_s, k.n_s)
-    need("w_si")
-    k.sqkv[...] = (dot_nt(k.n_s[...], k.w_si[...]) + qkv_row("s_qv")).astype(BHALF)
-    in_frame = jnp.where(iota((1, ROWS), 1) < patches + 1, 0.0, NEG)
-    for f in range(frames):
-        k.att_s[0, c, frame(f), :] = attend_all(k.sqkv[frame(f), :], in_frame, k.p_s, f * heads)
+        norm(k.x32, 1, s_gain, s_beta, k.xh_s, k.n_s, r)
+        k.sqkv[r, :] = (dot_nt(k.n_s[r, :], k.w_si[...]) + s_qb).astype(BHALF)
+        k.att_s[0, c, r, :] = attend_all(k.sqkv[r, :], in_frame, k.p_s, f * heads)
+        sa_copies.append(features(f, k.att_s))
     arrived([w_so_near, w_so_last])
-    project(k.att_s, k.w_so)
-    s_ob = vec("s_ob")
+    s_ob, m_gain, m_beta = vec("s_ob"), vec("m_gain"), vec("m_beta")
+    for f in range(frames):
+        own_part(f, k.att_s, k.w_so, sa_copies[f])
+    sa_last = []
+    for f in range(frames):
+        sa_last.append(features_on(f, k.att_s, sa_copies[f]))
     cls_at = [slice(f * ROWS + patches, f * ROWS + patches + 1) for f in range(frames)]
-    space_cls = [k.t32[r, :] + k.u32[r, :] + s_ob for r in cls_at]
+    space_cls = []
+    for f in range(frames):
+        r = frame(f)
+        k.t32[r, :] = both_parts(f, k.att_s, k.w_so, sa_last[f]) + s_ob
+        space_cls.append(k.t32[cls_at[f], :])
+        k.x32[r, :] = k.x32[r, :] + k.t32[r, :]
+        set_tail(k.x32, f, [])
     parts = [sum(onehot[f][i] * space_cls[f] for f in range(frames)) for i in range(clips)]
     k.cls_send[...] = eight(parts)
-    cls_copies = [send(k.cls_send, k.cls_recv.at[s], (p, h)) for p in peers]
+    cls_copies = [send(k.cls_send, k.cls_recv.at[s], (p, h), k.cls_recv.at[q]) for p, q in zip(peers, givers)]
     k.cls_recv[s] = k.cls_send[...]
 
-    def add_space(r):
-        k.x32[r, :] = k.x32[r, :] + (k.t32[r, :] + k.u32[r, :] + s_ob)
-
-    blocks(add_space)
-    for f in range(frames):
-        set_tail(k.x32, f, [])
-
-    m_gain, m_beta = vec("m_gain"), vec("m_beta")
-    norm(k.x32, 2, m_gain, m_beta, k.xh_m, k.n_m)
-    need("w_up")
-    k.t32[...] = dot_nn(k.n_m[...], k.w_up[...])
-    arrived(cls_copies)
-    cls_sum = k.cls_recv[0]
-    for i in range(1, seq):
-        cls_sum = cls_sum + k.cls_recv[i]
-    set_tail(k.x32, 0, [cls32[i : i + 1] + cls_sum[i : i + 1] * per_len[i] for i in range(clips)])
-    last_block = slice(ROWS - HALF, ROWS)
-    norm_rows(k.x32, 2, m_gain, m_beta, k.xh_m, k.n_m, last_block)
-    k.t32[last_block, :] = dot_nn(k.n_m[last_block, :], k.w_up[...])
     first_seq = jnp.where(s == 0, 1.0, 0.0)
     m_ub = vec("m_ub")
+    need("w_up")
+
+    def up_rows(r):
+        norm(k.x32, 2, m_gain, m_beta, k.xh_m, k.n_m, r)
+        k.t32[r, :] = dot_nn(k.n_m[r, :], k.w_up[...])
 
     def kept(r):
-        at = r.start + iota((BLOCK, 1), 0)
+        at = r.start + iota((r.stop - r.start, 1), 0)
         return jnp.where((at >= patches) & (at < ROWS), first_seq, 1.0)
 
     def gelu_rows(r):
@@ -915,66 +908,92 @@
         slope = cdf + pre * jnp.exp(-0.5 * pre * pre) * 0.3989422804014327
         act = pre * cdf
         grad = k.dact[r, :] * slope
-        keep = kept(r)
         k.act[r, :] = act.astype(BHALF)
-        k.act_k[r, :] = (act * keep).astype(BHALF)
         k.gpre[r, :] = grad.astype(BHALF)
-        k.gpre_k[r, :] = (grad * keep).astype(BHALF)
-
-    blocks(gelu_rows)
-
-    def sum_make(i, lhs, rhs, dot):
+        if r.start == 0:
+            act, grad = act * kept(r), grad * kept(r)
+        k.act_k[r, :] = act.astype(BHALF)
+        k.gpre_k[r, :] = grad.astype(BHALF)
+
+    def sum_open(i, f, lhs, rhs, dot):
+        r = frame(f)
         for b in range(2):
             cut = slice(b * half, (b + 1) * half)
-            k.part[i, b] = dot(lhs[...], rhs[cut, :] if dot is dot_nt else rhs[:, cut]).astype(BHALF)
-
-    def sum_open(i):
-        return send(k.part.at[i, other_c], k.pair.at[i], sister)
-
-    def sum_across(i, copy):
+            k.part[i, b, r, :] = dot(lhs[r, :], rhs[cut, :] if dot is dot_nt else rhs[:, cut]).astype(BHALF)
+        return send(k.part.at[i, other_c, r], k.pair.at[i, r], sister, k.pair.at[i, r])
+
+    def sum_across(i, f, copy):
+        r = frame(f)
         copy.wait_recv()
-        k.part[i, c] = (k.part[i, c].astype(FLOAT) + k.pair[i].astype(FLOAT)).astype(BHALF)
-        return send(k.part.at[i, c], k.other.at[i], across)
-
-    def sum_close(i, copy):
+        k.part[i, c, r, :] = (k.part[i, c, r, :].astype(FLOAT) + k.pair[i, r, :].astype(FLOAT)).astype(BHALF)
+        return send(k.part.at[i, c, r], k.other.at[i, r], across, k.other.at[i, r])
+
+    def sum_close(i, f, copy):
+        r = frame(f)
         copy.wait_recv()
-        k.total[i, c] = (k.part[i, c].astype(FLOAT) + k.other[i].astype(FLOAT)).astype(BHALF)
-        return send(k.total.at[i, c], k.total.at[i, c], sister)
-
-    def rows_of(ref, r):
-        return jnp.concatenate([ref[0, r, :], ref[1, r, :]], axis=-1).astype(FLOAT)
-
-    def grad_make(name, lhs, rhs):
+        k.total[i, c, r, :] = (k.part[i, c, r, :].astype(FLOAT) + k.other[i, r, :].astype(FLOAT)).astype(BHALF)
+        return send(k.total.at[i, c, r], k.total.at[i, c, r], sister, k.total.at[i, other_c, r])
+
+    def rows_of(ref, i, r):
+        return jnp.concatenate([ref[i, 0, r, :], ref[i, 1, r, :]], axis=-1).astype(FLOAT)
+
+    z_hi, z_lo = z // 2, z % 2
+    z_near, z_far = ((z + 1 - 2 * z_lo) * 2 + y, h), (((z + 2) % zs) * 2 + y, h)
+    z_first = ("up", "l", "tb")
+
+    def grad_make(name, *pairs):
         g = getattr(k, "g_" + name)
-        g[...] = dot_tn(lhs, rhs).astype(BHALF).reshape(g.shape)
+        parts = [dot_tn(lhs, rhs).astype(BHALF) for lhs, rhs in pairs]
+        value = parts[0] if len(parts) == 1 else jnp.concatenate(parts, axis=-1)
+        g[...] = value.reshape(g.shape)
+
+    class Reduction:
+        def __init__(self, name):
+            self.name, self.g = name, getattr(k, "g_" + name)
+            self.first, self.second, self.third = [getattr(k, kind + name) for kind in ("y_", "z_", "x_")]
+            ways = [(y, y_peer), (z_lo, z_near)]
+            (self.one, self.peer_one), (self.two, self.peer_two) = ways[::-1] if name in z_first else ways
+
+        def at(self, one, two):
+            return (slice(None), one, two) if self.name in z_first else (slice(None), two, one)
+
+        def add(self, at, got):
+            self.g[at] = (self.g[at].astype(FLOAT) + got.astype(FLOAT)).astype(BHALF)
 
     def grad_open(name):
-        g, got = getattr(k, "g_" + name), getattr(k, "y_" + name)
-        return name, [send(g.at[p, 1 - y], got.at[p], y_peer) for p in z_peers + [z]]
-
-    def grad_along(job):
-        name, opened = job
-        g, got, last = [getattr(k, kind + name) for kind in ("g_", "y_", "z_")]
-        copies = []
-        for p, copy in zip(z_peers, opened):
-            copy.wait_recv()
-            g[p, y] = (g[p, y].astype(FLOAT) + got[p].astype(FLOAT)).astype(BHALF)
-            copies.append(send(g.at[p, y], last.at[z], (p * 2 + y, h)))
-        opened[-1].wait_recv()
-        last[z] = (g[z, y].astype(FLOAT) + got[z].astype(FLOAT)).astype(BHALF)
-        return name, copies
+        job = Reduction(name)
+        job.copies = []
+        for two in (1 - job.two, job.two):
+            into = job.first.at[two]
+            job.copies.append(send(job.g.at[job.at(1 - job.one, two)], into, job.peer_one, into))
+        return job
+
+    def grad_near(job):
+        job.copies[0].wait_recv()
+        away, kept_here = job.at(job.one, 1 - job.two), job.at(job.one, job.two)
+        job.add(away, job.first[1 - job.two])
+        copy = send(job.g.at[away], job.second, job.peer_two, job.second)
+        job.copies[1].wait_recv()
+        job.add(kept_here, job.first[job.two])
+        job.copies = [copy]
+        return job
+
+    def grad_far(job):
+        job.copies[0].wait_recv()
+        job.add(job.at(job.one, job.two), job.second[...])
+        job.copies = [send(job.g.at[1 - z_hi, z_lo, y], job.third, z_far, job.third)]
+        return job
 
     def grad_close(job):
-        name, copies = job
-        last, out = getattr(k, "z_" + name), getattr(k, "o_" + name)
-        arrived(copies)
-        out[...] = sum(last[i].astype(FLOAT) for i in range(zs))
+        job.copies[0].wait_recv()
+        getattr(k, "o_" + job.name)[...] = job.g[z_hi, z_lo, y].astype(FLOAT) + job.third[...].astype(FLOAT)
 
     def vectors_send(which, values):
         value = eight(values)
         k.v_send[which] = value
         k.v_recv[which, s] = value
-        return [send(k.v_send.at[which], k.v_recv.at[which, s], (p, h)) for p in peers]
+        into = k.v_recv.at[which]
+        return [send(k.v_send.at[which], into.at[s], (p, h), into.at[q]) for p, q in zip(peers, givers)]
 
     def vectors_close(which, copies):
         arrived(copies)
@@ -993,160 +1012,174 @@
             out = jnp.concatenate([out, jnp.zeros((1, model - out.shape[1]), FLOAT)], axis=-1)
         return out
 
-    def block_sums(body):
-        def step(b, sums):
-            pair = body(pl.ds(pl.multiple_of(b * BLOCK, BLOCK), BLOCK))
-            return tuple(t + jnp.sum(v.reshape(BLOCK // 8, 8, model), axis=0) for t, v in zip(sums, pair))
-
-        zero = jnp.zeros((8, model), FLOAT)
-        sums = lax.fori_loop(0, rows // BLOCK, step, (zero, zero))
-        return [jnp.sum(v, axis=0, keepdims=True) for v in sums]
-
-    def norm_back(i, which, gain, xhat, keep, use):
-        def body(r):
-            g = rows_of(k.total.at[i], r)
-            n = xhat[r, :]
-            gh = g * gain
-            m1 = jnp.mean(gh, axis=-1, keepdims=True)
-            m2 = jnp.mean(gh * n, axis=-1, keepdims=True)
-            use(r, k.inv[which, r, 0:1] * (gh - m1 - n * m2))
-            w = g * kept(r) if keep else g
-            return w * n, w
-
-        return block_sums(body)
-
-    sum_make(0, k.gpre, k.w_up, dot_nt)
-    m_sum = sum_open(0)
-    grad_make("dn", k.gr16[...], k.act_k[...])
-    m_sum = sum_across(0, m_sum)
+    def column_sum(v):
+        return jnp.sum(v, axis=0, keepdims=True)
+
+    def add_all(lists):
+        return [sum(v) for v in zip(*lists)]
+
+    def norm_back(i, which, gain, xhat, r, keep):
+        g = rows_of(k.total, i, r)
+        n = xhat[r, :]
+        gh = g * gain
+        m1 = jnp.mean(gh, axis=-1, keepdims=True)
+        m2 = jnp.mean(gh * n, axis=-1, keepdims=True)
+        dx = k.inv[which, r, 0:1] * (gh - m1 - n * m2)
+        w = g * kept(r) if keep and r.start == 0 else g
+        return dx, (column_sum(w * n), column_sum(w))
+
+    m_sum = [None] * frames
+    for f in range(1, frames):
+        up_rows(frame(f))
+        gelu_rows(frame(f))
+        m_sum[f] = sum_open(0, f, k.gpre, k.w_up, dot_nt)
+    up_rows(frame(0))
+    for f in range(1, frames):
+        m_sum[f] = sum_across(0, f, m_sum[f])
+    arrived(cls_copies)
+    cls_sum = k.cls_recv[0]
+    for i in range(1, seq):
+        cls_sum = cls_sum + k.cls_recv[i]
+    set_tail(k.x32, 0, [cls32[i : i + 1] + cls_sum[i : i + 1] * per_len[i] for i in range(clips)])
+    up_rows(slice(ROWS - HALF, ROWS))
+    gelu_rows(frame(0))
+    m_sum[0] = sum_open(0, 0, k.gpre, k.w_up, dot_nt)
+    o_sum = [sum_open(1, f, k.act, k.w_dn, dot_nn) for f in range(frames)]
+    m_sum[0] = sum_across(0, 0, m_sum[0])
+    grad_make("dn", (k.gr16[...], k.act_k[...]))
     j_dn = grad_open("dn")
-    grad_make("up", k.n_m[...], k.gpre_k[...])
+    grad_make("up", (k.n_m[...], k.gpre_k[...]))
     j_up = grad_open("up")
-    sum_make(1, k.act, k.w_dn, dot_nn)
-    o_sum = sum_open(1)
     ub_grad, db_grad = col_sums(k.gpre_k), col_sums(k.gr16, ones_kept)
-    m_last = sum_close(0, m_sum)
-    o_sum = sum_across(1, o_sum)
-    m_last.wait_recv()
-
-    def use_m(r, dx):
-        k.gr32[r, :] = k.gr32[r, :] + dx
-
-    sums = norm_back(0, 2, m_gain, k.xh_m, True, use_m)
-    v_m = vectors_send(0, [sums[0], sums[1], ub_grad, db_grad])
+    m_last, sums = [None] * frames, [None] * frames
+    backwards = list(range(1, frames)) + [0]
+    for f in backwards:
+        m_last[f] = sum_close(0, f, m_sum[f])
+    for f in backwards:
+        m_last[f].wait_recv()
+        dx, sums[f] = norm_back(0, 2, m_gain, k.xh_m, frame(f), True)
+        k.gr32[frame(f), :] = k.gr32[frame(f), :] + dx
     grad_cls_mid = k.gr32[patches : patches + clips, :]
     k.gcm[...] = eight([grad_cls_mid])
-    for f in range(frames):
-        shared = sum(onehot[f][i] * (grad_cls_mid[i : i + 1] * per_len[i]) for i in range(clips))
-        set_tail(k.gr32, f, [shared])
-    cast_rows(k.gr32, k.gss)
-    for f in range(frames):
+    shares = [
+        sum(onehot[f][i] * (grad_cls_mid[i : i + 1] * per_len[i]) for i in range(clips)) for f in range(frames)
+    ]
+
+    def space_back(f):
+        r = frame(f)
+        set_tail(k.gr32, f, [shares[f]])
+        k.gss[r, :] = k.gr32[r, :].astype(BHALF)
         set_tail(k.gr32, f, [])
-
-    k.gatt[...] = dot_nt(k.gss[...], k.w_so[0, c]).astype(BHALF)
-    for f in range(frames):
-        k.dsq[frame(f), :] = attend_back_all(k.sqkv[frame(f), :], k.gatt[frame(f), :], k.p_s, f * heads)
-    sum_make(2, k.dsq, k.w_si, dot_nn)
-    s_sum = sum_open(2)
-    j_dn = grad_along(j_dn)
-    s_sum = sum_across(2, s_sum)
-    grad_make("si", k.n_s[...], k.dsq[...])
-    j_si = grad_open("si")
-    grad_make("so", k.gss[...], k.att_s[0, c])
-    j_so = grad_open("so")
-    o_last = sum_close(1, o_sum)
+        grad = dot_nt(k.gss[r, :], k.w_so[0, c]).astype(BHALF)
+        k.dsq[r, :] = attend_back_all(k.sqkv[r, :], grad, k.p_s, f * heads)
+        return sum_open(2, f, k.dsq, k.w_si, dot_nn)
+
+    s_sum = []
+    for f in range(frames):
+        s_sum.append(space_back(f))
+        if f:
+            s_sum[f - 1] = sum_across(2, f - 1, s_sum[f - 1])
+    m_rows = add_all(sums) + [ub_grad, db_grad]
+    s_sum[-1] = sum_across(2, frames - 1, s_sum[-1])
+    j_dn = grad_near(j_dn)
+    j_up = grad_near(j_up)
+    v_m = vectors_send(0, m_rows)
+    grad_make("s", (k.n_s[...], k.dsq[...]), (k.gss[...], k.att_s[0, c]))
+    j_s = grad_open("s")
     s_rows = [col_sums(k.gss), col_sums(k.dsq)]
-    j_up = grad_along(j_up)
-    o_last.wait_recv()
-    m_db = vec("m_db")
-
-    def out_rows(r):
-        k.t32[r, :] = k.x32[r, :] + rows_of(k.total.at[1], r) + m_db
-
-    blocks(out_rows)
-    for f in range(frames):
-        k.o_blk[:, f, :] = k.t32[f * ROWS : f * ROWS + patches, :].astype(BHALF)
-    k.o_cls[...] = k.t32[patches : patches + clips, :].astype(BHALF)
-    s_last = sum_close(2, s_sum)
-    s_last.wait_recv()
-    sums = norm_back(2, 1, s_gain, k.xh_s, False, use_m)
-    cls_in = [k.gr32[r, :] for r in cls_at]
-    cls_parts = [sum(onehot[f][i] * cls_in[f] for f in range(frames)) for i in range(clips)]
-    for f in range(frames):
+    s_last = [sum_close(2, f, s_sum[f]) for f in range(frames)]
+
+    g_copies, cls_in = [], []
+    for f in range(frames):
+        r = frame(f)
+        s_last[f].wait_recv()
+        dx, sums[f] = norm_back(2, 1, s_gain, k.xh_s, r, False)
+        k.gr32[r, :] = k.gr32[r, :] + dx
+        cls_in.append(k.gr32[cls_at[f], :])
         set_tail(k.gr32, f, [])
-    cast_rows(k.gr32, k.gtr)
-
-    k.gtm[...] = dot_nt(k.gtr[...], k.w_tl[...]).astype(BHALF)
-    k.gatt[...] = dot_nt(k.gtm[...], k.w_to[0, c]).astype(BHALF)
-    g_copies = []
-    for f in range(frames):
-        g_copies += scatter(f, k.gatt[frame(f), :], k.g_send, k.g_pos)
-    v_s = vectors_send(1, [sums[0], sums[1]] + s_rows + cls_parts)
+        k.gtr[r, :] = k.gr32[r, :].astype(BHALF)
+        k.gtm[r, :] = dot_nt(k.gtr[r, :], k.w_tl[...]).astype(BHALF)
+        grad = dot_nt(k.gtm[r, :], k.w_to[0, c]).astype(BHALF)
+        g_copies.append(scatter(f, grad, k.g_send, k.g_pos))
+    o_sum = [sum_across(1, f, o_sum[f]) for f in range(frames)]
+    j_dn = grad_far(j_dn)
+    j_up = grad_far(j_up)
     pick = (iota((model, width), 0) == h * width + iota((model, width), 1)).astype(FLOAT).astype(BHALF)
-    grad_make("tl", k.mid16[...], dot_nn(k.gtr[...], pick).astype(BHALF))
-    grad_make("to", k.gtm[...], k.att_t[0, c])
-    t_rows = [col_sums(k.gtm), col_sums(k.gtr)]
-    arrived(g_copies)
+    grad_make("l", (k.mid16[...], dot_nn(k.gtr[...], pick).astype(BHALF)), (k.gtm[...], k.att_t[0, c]))
+    j_l = grad_open("l")
     d_copies = []
     for b in range(2):
-        value = attend_back_all(
+        for copies in g_copies:
+            arrived(copies[b])
+            value = attend_back_all(
             k.q_pos[b].reshape(span, 3 * width), k.g_pos[b].reshape(span, width), k.p_t, b * heads
         )
         k.d_pos[b] = value.reshape(every, HALF, 3 * width)
         d_copies += gather(b, k.d_pos, k.d_recv)
-    j_tl = grad_open("tl")
-    j_to = grad_open("to")
-    j_si = grad_along(j_si)
-    j_so = grad_along(j_so)
+    j_s = grad_near(j_s)
+    cls_parts = [sum(onehot[f][i] * cls_in[f] for f in range(frames)) for i in range(clips)]
+    v_s = vectors_send(1, add_all(sums) + s_rows + cls_parts)
+    t_rows = [col_sums(k.gtm), col_sums(k.gtr)]
+    o_last = [sum_close(1, f, o_sum[f]) for f in range(frames)]
+    m_vec = vectors_close(0, v_m)
+    k.o_vec[0:8, :] = m_vec
+    m_db = vec("m_db")
+    for f in range(frames):
+        r = frame(f)
+        o_last[f].wait_recv()
+        out = k.x32[r, :] + rows_of(k.total, 1, r) + m_db
+        k.o_blk[:, f, :] = out[:patches].astype(BHALF)
+        if f == 0:
+            k.o_cls[...] = out[patches : patches + clips].astype(BHALF)
     grad_close(j_dn)
-    m_vec = vectors_close(0, v_m)
+    grad_close(j_up)
+    j_l = grad_near(j_l)
+    arrived(d_copies)
+    t_sum, shared = [], []
+    for f in range(frames):
+        k.dtq[frame(f), :] = gathered(f, k.d_recv)
+        t_sum.append(sum_open(3, f, k.dtq, k.w_ti, dot_nn))
+    grad_make("ta", (k.n_t[...], k.dtq[:, : 2 * width]))
+    j_ta = grad_open("ta")
+    for f in range(frames):
+        g = rows_of(k.part, 3, frame(f))
+        shared.append((column_sum(g * k.xh_t[frame(f), :]), column_sum(g)))
+        t_sum[f] = sum_across(3, f, t_sum[f])
+    grad_make("tb", (k.n_t[...], k.dtq[:, 2 * width :]))
+    j_tb = grad_open("tb")
+    v_t = vectors_send(2, add_all(shared) + [t_rows[0], col_sums(k.dtq), t_rows[1]])
+    j_s = grad_far(j_s)
     s_vec = vectors_close(1, v_s)
-    k.o_vec[0:8, :] = m_vec
     k.o_vec[8:16, :] = s_vec + jnp.concatenate([jnp.zeros((4, model), FLOAT), k.gcm[0:4, :]], axis=0)
-    arrived(d_copies)
-    for f in range(frames):
-        k.dtq[frame(f), :] = gathered(f, k.d_recv)
-    sum_make(3, k.dtq, k.w_ti, dot_nn)
-    t_sum = sum_open(3)
-    grad_make("ti", k.n_t[...], k.dtq[...])
-    j_ti = grad_open("ti")
-
-    def partial(r):
-        g = rows_of(k.part.at[3], r)
-        return g * k.xh_t[r, :], g
-
-    sums = block_sums(partial)
-    t_sum = sum_across(3, t_sum)
-    v_t = vectors_send(2, [sums[0], sums[1], t_rows[0], col_sums(k.dtq), t_rows[1]])
-    j_tl = grad_along(j_tl)
-    j_to = grad_along(j_to)
-    grad_close(j_up)
-    grad_close(j_si)
-    grad_close(j_so)
+    j_l = grad_far(j_l)
+    j_ta = grad_near(j_ta)
+    t_last = [sum_close(3, 0, t_sum[0])]
     t_vec = vectors_close(2, v_t)
     k.v_head[h] = t_vec
-    h_copies = [send(k.v_head.at[h], k.v_head.at[h], device) for device in (sister, across, diagonal)]
-    j_ti = grad_along(j_ti)
-    t_last = sum_close(3, t_sum)
-    grad_close(j_tl)
-    grad_close(j_to)
-    t_last.wait_recv()
-
-    def use_t(r, dx):
-        k.t32[r, :] = k.gr32[r, :] + dx.astype(BHALF).astype(FLOAT)
-
-    norm_back(3, 0, t_gain, k.xh_t, False, use_t)
-    for f in range(frames):
-        k.o_tok[:, f, :] = k.t32[f * ROWS : f * ROWS + patches, :].astype(BHALF)
+    h_copies = [send(k.v_head.at[h], k.v_head.at[h], d, k.v_head.at[d[1]]) for d in (sister, across, diagonal)]
+    t_last += [sum_close(3, f, t_sum[f]) for f in range(1, frames)]
+    for f in range(frames):
+        r = frame(f)
+        t_last[f].wait_recv()
+        if f == 0:
+            j_tb = grad_near(j_tb)
+        dx, _ = norm_back(3, 0, t_gain, k.xh_t, r, False)
+        out = k.gr32[r, :] + dx.astype(BHALF).astype(FLOAT)
+        k.o_tok[:, f, :] = out[:patches].astype(BHALF)
+    j_ta = grad_far(j_ta)
+    grad_close(j_s)
     arrived(h_copies)
     over_head = k.v_head[0] + k.v_head[1] + k.v_head[2] + k.v_head[3]
     k.o_vec[16:24, :] = jnp.concatenate([over_head[0:2], t_vec[2:8]], axis=0)
-    grad_close(j_ti)
+    j_tb = grad_far(j_tb)
+    grad_close(j_l)
+    grad_close(j_ta)
+    grad_close(j_tb)
     for copy in unsent:
         copy.wait_send()
 
 
-def finish_kernel(dims, h_blk, h_tok, vec, cls_out, g_dn, g_up, g_si, g_so, g_tl, g_to, g_ti, *refs):
+def finish_kernel(dims, h_blk, h_tok, vec, cls_out, g_dn, g_up, g_s, g_l, g_ta, g_tb, *refs):
     width, model, seq = dims["width"], dims["model"], dims["seq"]
     share, clips = model // seq, dims["clips"]
     o_blk, o_cls, o_tok, cls, tg, tb, ti, tp, to, tob, tl, tlb, sg, sb, si, sp, so, sob, mg, mb, up, ub, dn, db = refs
@@ -1164,14 +1197,14 @@
     for out, row in ((sp, 11), (tp, 19)):
         out[0:1, :] = v[row : row + 1, :width]
         out[1:2, :] = v[row : row + 1, 2 * width : 3 * width]
-    for out, g in ((si, g_si), (ti, g_ti)):
-        for i in range(3):
-            out[i] = g[:, i * width : (i + 1) * width]
-    tl[...] = g_tl[...]
+    for i in range(3):
+        si[i] = g_s[:, i * width : (i + 1) * width]
+    ti[0], ti[1], ti[2] = g_ta[:, :width], g_ta[:, width:], g_tb[...]
+    tl[...] = g_l[:, :width]
     up[...] = g_up[...]
     dn[...] = g_dn[...]
-    to[...] = g_to[...].T
-    so[...] = g_so[...].T
+    to[...] = g_l[:, width:].T
+    so[...] = g_s[:, 3 * width :].T
 
 
 def fused_body(
@@ -1213,7 +1246,6 @@
         hidden=hidden,
         clips=clips,
         pos=-(-patches // seq),
-        unroll=False,
     )
 
     def frames_inner(v):
@@ -1304,7 +1336,7 @@
     last = pl.pallas_call(
         functools.partial(finish_kernel, dims),
         out_shape=out_shape,
-        in_specs=[vmem] * 11,
+        in_specs=[vmem] * 10,
         out_specs=[vmem] * len(out_shape),
         compiler_params=pltpu.CompilerParams(vmem_limit_bytes=62 * 1024 * 1024),
         name="finish",

time: 180 us -> 152 us (0.84)
  Pallas kernels: 179 us -> 151 us
    pallas_call x1, Pallas kernels: 176 us -> 148 us  [fused_body(): pl.pallas_call(functools.partial(layer_kernel, dims, names), out_shape=ou...]
where the time goes in v3:
time: 152 us
  Pallas kernels  151 us (99%)
    pallas_call x1, Pallas kernels, fused_body(): pl.pallas_call(functools.partial(layer_kernel, dims, names), out_shape=ou...  148 us
    pallas_call x1, Pallas kernels, fused_body(): pl.pallas_call(functools.partial(finish_kernel, dims), out_shape=out_shap...  3.5 us

profile of v3, /device:TPU:0, one launch (start us, length us, event | category | flops | bytes accessed | tf_op | source)
XLA Modules:
  0.0 152.1 jit_solution(8663623958260106052)
XLA Ops:
  0.7 147.8 %layer.1 = (bf16[196,2,768]{2,1,0:T(2,128)(2,1)}, bf16[4,768]{1,0:T(4,128)(2,1)}, bf16[196,2,768]{2,1,0:T(2,128)(2,1)}, f32[24,768]{1,0:T(8,128)}, f32[96,768]{1...) custom-call(s32[4]{0:T(128)} %refs_0_.1, ...), custom_call_target="tpu_custom_call" | custom-call | tf_op jit(solution)/shard_map/layer/pallas_call | solution.py:1270
  148.5 3.5 %finish.1 = (bf16[196,2,768]{2,1,0:T(2,128)(2,1)}, bf16[4,768]{1,0:T(4,128)(2,1)}, bf16[196,2,768]{2,1,0:T(2,128)(2,1)}, f32[4,96]{1,0:T(4,128)}, f32[96]{0:T(12...) custom-call(bf16[196,2,768]{2,1,0:T(2,128)(2,1)} %get-tuple-element., ...), custom_call_target="tpu_custom_call" | custom-call | tf_op jit(solution)/shard_map/finish/pallas_call | solution.py:1336

commit v4 on v3

--- a/solution.py
+++ b/solution.py
@@ -547,8 +547,9 @@
         pair=vm((4, rows, half), low),
         other=vm((4, rows, half), low),
         total=vm((4, 2, rows, half), low),
-        cls_send=vm((8, model), FLOAT),
-        cls_recv=vm((seq, 8, model), FLOAT),
+        cls_send=vm((8, width), FLOAT),
+        cls_recv=vm((seq, 8, width), FLOAT),
+        cls_head=vm((4, 8, model), FLOAT),
         gcm=vm((8, model), FLOAT),
         v_send=vm((3, 8, model), FLOAT),
         v_recv=vm((3, seq, 8, model), FLOAT),
@@ -565,8 +566,8 @@
     for name in PAIRS:
         shapes[name] = vm((2, width), FLOAT)
     shapes["load"] = pltpu.SemaphoreType.DMA((32,))
-    shapes["sent"] = pltpu.SemaphoreType.DMA((280,))
-    shapes["got"] = pltpu.SemaphoreType.DMA((280,))
+    shapes["sent"] = pltpu.SemaphoreType.DMA((320,))
+    shapes["got"] = pltpu.SemaphoreType.DMA((320,))
     return shapes
 
 
@@ -695,7 +696,7 @@
 
     def eight(values):
         missing = 8 - sum(v.shape[0] for v in values)
-        fill = [jnp.zeros((missing, model), FLOAT)] if missing else []
+        fill = [jnp.zeros((missing, values[0].shape[1]), FLOAT)] if missing else []
         return jnp.concatenate(list(values) + fill, axis=0)
 
     def frame(f):
@@ -714,9 +715,12 @@
         for copy in copies:
             copy.wait_recv()
 
-    def scatter(f, value, src, dst):
+    def to_slots(f, value, src):
         moved = dot_nn(k.sel[...], value).astype(BHALF)
         src[f] = moved.reshape(seq, 2, HALF, value.shape[-1])
+
+    def scatter(f, value, src, dst):
+        to_slots(f, value, src)
         to = frames * s + f
         copies = [
             [send(src.at[f, p, b], dst.at[b, to], (p, h), dst.at[b, frames * q + f]) for p, q in zip(peers, givers)]
@@ -870,6 +874,14 @@
         k.sqkv[r, :] = (dot_nt(k.n_s[r, :], k.w_si[...]) + s_qb).astype(BHALF)
         k.att_s[0, c, r, :] = attend_all(k.sqkv[r, :], in_frame, k.p_s, f * heads)
         sa_copies.append(features(f, k.att_s))
+    lone = patches - (ROWS - HALF)
+    feats = []
+    for f in range(frames):
+        last_rows = k.att_s[0, c, (f + 1) * ROWS - HALF : (f + 1) * ROWS, :].astype(FLOAT)
+        feats.append(last_rows[lone : lone + 1])
+    k.cls_send[...] = eight([sum(onehot[f][i][:, :width] * feats[f] for f in range(frames)) for i in range(clips)])
+    cls_copies = [send(k.cls_send, k.cls_recv.at[s], (p, h), k.cls_recv.at[q]) for p, q in zip(peers, givers)]
+    k.cls_recv[s] = k.cls_send[...]
     arrived([w_so_near, w_so_last])
     s_ob, m_gain, m_beta = vec("s_ob"), vec("m_gain"), vec("m_beta")
     for f in range(frames):
@@ -877,18 +889,19 @@
     sa_last = []
     for f in range(frames):
         sa_last.append(features_on(f, k.att_s, sa_copies[f]))
+    arrived(cls_copies)
+    feat = k.cls_recv[0]
+    for i in range(1, seq):
+        feat = feat + k.cls_recv[i]
+    high = feat.astype(BHALF)
+    rest = (feat - high.astype(FLOAT)).astype(BHALF)
+    k.cls_head[h] = dot_nn(high, k.w_so[0, c]) + dot_nn(rest, k.w_so[0, c])
+    cls_copies = [send(k.cls_head.at[h], k.cls_head.at[h], d, k.cls_head.at[d[1]]) for d in (sister, across, diagonal)]
     cls_at = [slice(f * ROWS + patches, f * ROWS + patches + 1) for f in range(frames)]
-    space_cls = []
     for f in range(frames):
         r = frame(f)
-        k.t32[r, :] = both_parts(f, k.att_s, k.w_so, sa_last[f]) + s_ob
-        space_cls.append(k.t32[cls_at[f], :])
-        k.x32[r, :] = k.x32[r, :] + k.t32[r, :]
+        k.x32[r, :] = k.x32[r, :] + (both_parts(f, k.att_s, k.w_so, sa_last[f]) + s_ob)
         set_tail(k.x32, f, [])
-    parts = [sum(onehot[f][i] * space_cls[f] for f in range(frames)) for i in range(clips)]
-    k.cls_send[...] = eight(parts)
-    cls_copies = [send(k.cls_send, k.cls_recv.at[s], (p, h), k.cls_recv.at[q]) for p, q in zip(peers, givers)]
-    k.cls_recv[s] = k.cls_send[...]
 
     first_seq = jnp.where(s == 0, 1.0, 0.0)
     m_ub = vec("m_ub")
@@ -939,7 +952,7 @@
 
     z_hi, z_lo = z // 2, z % 2
     z_near, z_far = ((z + 1 - 2 * z_lo) * 2 + y, h), (((z + 2) % zs) * 2 + y, h)
-    z_first = ("up", "l", "tb")
+    z_first = ('up',)
 
     def grad_make(name, *pairs):
         g = getattr(k, "g_" + name)
@@ -1037,10 +1050,8 @@
     for f in range(1, frames):
         m_sum[f] = sum_across(0, f, m_sum[f])
     arrived(cls_copies)
-    cls_sum = k.cls_recv[0]
-    for i in range(1, seq):
-        cls_sum = cls_sum + k.cls_recv[i]
-    set_tail(k.x32, 0, [cls32[i : i + 1] + cls_sum[i : i + 1] * per_len[i] for i in range(clips)])
+    cls_sum = k.cls_head[0] + k.cls_head[1] + k.cls_head[2] + k.cls_head[3]
+    set_tail(k.x32, 0, [cls32[i : i + 1] + cls_sum[i : i + 1] * per_len[i] + s_ob for i in range(clips)])
     up_rows(slice(ROWS - HALF, ROWS))
     gelu_rows(frame(0))
     m_sum[0] = sum_open(0, 0, k.gpre, k.w_up, dot_nt)
@@ -1167,12 +1178,12 @@
         out = k.gr32[r, :] + dx.astype(BHALF).astype(FLOAT)
         k.o_tok[:, f, :] = out[:patches].astype(BHALF)
     j_ta = grad_far(j_ta)
+    j_tb = grad_far(j_tb)
     grad_close(j_s)
+    grad_close(j_l)
     arrived(h_copies)
     over_head = k.v_head[0] + k.v_head[1] + k.v_head[2] + k.v_head[3]
     k.o_vec[16:24, :] = jnp.concatenate([over_head[0:2], t_vec[2:8]], axis=0)
-    j_tb = grad_far(j_tb)
-    grad_close(j_l)
     grad_close(j_ta)
     grad_close(j_tb)
     for copy in unsent:

time: 152 us -> 148 us (0.974)
  Pallas kernels: 151 us -> 147 us
    pallas_call x1, Pallas kernels: 148 us -> 143 us  [fused_body(): pl.pallas_call(functools.partial(layer_kernel, dims, names), out_shape=ou...]
where the time goes in v4:
time: 148 us; the launch traced here: 147 us
  Pallas kernels  147 us (99%)
    pallas_call x1, Pallas kernels, fused_body(): pl.pallas_call(functools.partial(layer_kernel, dims, names), out_shape=ou...  143 us
    pallas_call x1, Pallas kernels, fused_body(): pl.pallas_call(functools.partial(finish_kernel, dims), out_shape=out_shap...  3.5 us

profile of v4, /device:TPU:0, one launch (start us, length us, event | category | flops | bytes accessed | tf_op | source)
XLA Modules:
  0.0 147.4 jit_solution(667387988910495812)
XLA Ops:
  0.7 143.0 %layer.1 = (bf16[196,2,768]{2,1,0:T(2,128)(2,1)}, bf16[4,768]{1,0:T(4,128)(2,1)}, bf16[196,2,768]{2,1,0:T(2,128)(2,1)}, f32[24,768]{1,0:T(8,128)}, f32[96,768]{1...) custom-call(s32[4]{0:T(128)} %refs_0_.1, ...), custom_call_target="tpu_custom_call" | custom-call | tf_op jit(solution)/shard_map/layer/pallas_call | solution.py:1281
  143.7 3.5 %finish.1 = (bf16[196,2,768]{2,1,0:T(2,128)(2,1)}, bf16[4,768]{1,0:T(4,128)(2,1)}, bf16[196,2,768]{2,1,0:T(2,128)(2,1)}, f32[4,96]{1,0:T(4,128)}, f32[96]{0:T(12...) custom-call(bf16[196,2,768]{2,1,0:T(2,128)(2,1)} %get-tuple-element., ...), custom_call_target="tpu_custom_call" | custom-call | tf_op jit(solution)/shard_map/finish/pallas_call | solution.py:1347

commit v5 on v4

--- a/solution.py
+++ b/solution.py
@@ -1100,6 +1100,7 @@
     s_rows = [col_sums(k.gss), col_sums(k.dsq)]
     s_last = [sum_close(2, f, s_sum[f]) for f in range(frames)]
 
+    old = len(unsent)
     g_copies, cls_in = [], []
     for f in range(frames):
         r = frame(f)
@@ -1118,6 +1119,7 @@
     pick = (iota((model, width), 0) == h * width + iota((model, width), 1)).astype(FLOAT).astype(BHALF)
     grad_make("l", (k.mid16[...], dot_nn(k.gtr[...], pick).astype(BHALF)), (k.gtm[...], k.att_t[0, c]))
     j_l = grad_open("l")
+    newer = len(unsent)
     d_copies = []
     for b in range(2):
         for copies in g_copies:
@@ -1145,6 +1147,8 @@
     grad_close(j_dn)
     grad_close(j_up)
     j_l = grad_near(j_l)
+    for copy in unsent[:old]:
+        copy.wait_send()
     arrived(d_copies)
     t_sum, shared = [], []
     for f in range(frames):
@@ -1159,6 +1163,8 @@
     grad_make("tb", (k.n_t[...], k.dtq[:, 2 * width :]))
     j_tb = grad_open("tb")
     v_t = vectors_send(2, add_all(shared) + [t_rows[0], col_sums(k.dtq), t_rows[1]])
+    for copy in unsent[old:newer]:
+        copy.wait_send()
     j_s = grad_far(j_s)
     s_vec = vectors_close(1, v_s)
     k.o_vec[8:16, :] = s_vec + jnp.concatenate([jnp.zeros((4, model), FLOAT), k.gcm[0:4, :]], axis=0)
@@ -1186,7 +1192,7 @@
     k.o_vec[16:24, :] = jnp.concatenate([over_head[0:2], t_vec[2:8]], axis=0)
     grad_close(j_ta)
     grad_close(j_tb)
-    for copy in unsent:
+    for copy in unsent[newer:]:
         copy.wait_send()
 
 

time: 148 us -> 147 us (level)
  no operation moved by 1% of the time
where the time goes in v5:
time: 147 us
  Pallas kernels  146 us (99%)
    pallas_call x1, Pallas kernels, fused_body(): pl.pallas_call(functools.partial(layer_kernel, dims, names), out_shape=ou...  143 us
    pallas_call x1, Pallas kernels, fused_body(): pl.pallas_call(functools.partial(finish_kernel, dims), out_shape=out_shap...  3.5 us

profile of v5, /device:TPU:0, one launch (start us, length us, event | category | flops | bytes accessed | tf_op | source)
XLA Modules:
  0.0 147.2 jit_solution(6658892474908658196)
XLA Ops:
  0.7 142.8 %layer.1 = (bf16[196,2,768]{2,1,0:T(2,128)(2,1)}, bf16[4,768]{1,0:T(4,128)(2,1)}, bf16[196,2,768]{2,1,0:T(2,128)(2,1)}, f32[24,768]{1,0:T(8,128)}, f32[96,768]{1...) custom-call(s32[4]{0:T(128)} %refs_0_.1, ...), custom_call_target="tpu_custom_call" | custom-call | tf_op jit(solution)/shard_map/layer/pallas_call | solution.py:1287
  143.5 3.5 %finish.1 = (bf16[196,2,768]{2,1,0:T(2,128)(2,1)}, bf16[4,768]{1,0:T(4,128)(2,1)}, bf16[196,2,768]{2,1,0:T(2,128)(2,1)}, f32[4,96]{1,0:T(4,128)}, f32[96]{0:T(12...) custom-call(bf16[196,2,768]{2,1,0:T(2,128)(2,1)} %get-tuple-element., ...), custom_call_target="tpu_custom_call" | custom-call | tf_op jit(solution)/shard_map/finish/pallas_call | solution.py:1353
